TPU v7x, 128 devices: a whole 4x4x4 slice. The times are simulated.
128 devices in a mesh: ctx: 8 (over x, z_lo), fsdp: 16 (over z_hi, y, core).
Axes of the slice: x: 4, y: 4, z: 4 (z_hi: 2, z_lo: 2; z = z_hi * 2 + z_lo), core: 2. Of those that a mesh axis runs over, the one named last changes fastest.
Arguments:
- tokens: bfloat16 [16, 2048, 640], P('fsdp', 'ctx'), may hold values from -6 to 6
- cotangent: bfloat16 [16, 2048, 640], P('fsdp', 'ctx'), may hold values from -6 to 6
- starts: int32 [16], P('fsdp'), may hold values from 1 to 255
- qkv_weight: float32 [640, 1536], P(('ctx', 'fsdp')), may hold values from -0.25 to 0.25
- qkv_first: float32 [640, 1536], P(('ctx', 'fsdp')), may hold values from -34.393674 to 34.393674
- qkv_second: float32 [640, 1536], P(('ctx', 'fsdp')), may hold values from 1726.8736 to 6881.28
- out_weight: float32 [1024, 640], P(('ctx', 'fsdp')), may hold values from -2 to 2
- out_first: float32 [1024, 640], P(('ctx', 'fsdp')), may hold values from -3.04 to 3.04
- out_second: float32 [1024, 640], P(('ctx', 'fsdp')), may hold values from 13.4912 to 53.76
- gate_up_weight: float32 [640, 4096], P(('ctx', 'fsdp')), may hold values from -0.25 to 0.25
- gate_up_first: float32 [640, 4096], P(('ctx', 'fsdp')), may hold values from -12.16 to 12.16
- gate_up_second: float32 [640, 4096], P(('ctx', 'fsdp')), may hold values from 215.8592 to 860.16
- down_weight: float32 [2048, 640], P(('ctx', 'fsdp')), may hold values from -0.125 to 0.125
- down_first: float32 [2048, 640], P(('ctx', 'fsdp')), may hold values from -19.85659 to 19.85659
- down_second: float32 [2048, 640], P(('ctx', 'fsdp')), may hold values from 575.5894 to 2293.62
- norm_gains: float32 [2, 640], P(None, ('ctx', 'fsdp')), may hold values from 0.25 to 1.75
- gains_first: float32 [2, 640], P(None, ('ctx', 'fsdp')), may hold values from -34.393674 to 34.393674
- gains_second: float32 [2, 640], P(None, ('ctx', 'fsdp')), may hold values from 1726.8736 to 6881.28
Outputs:
- layer_out: float32 [16, 2048, 640], P('fsdp', 'ctx')
- input_grad: float32 [16, 2048, 640], P('fsdp', 'ctx')
- next_qkv: float32 [640, 1536], P(('ctx', 'fsdp'))
- next_qkv_first: float32 [640, 1536], P(('ctx', 'fsdp'))
- next_qkv_second: float32 [640, 1536], P(('ctx', 'fsdp'))
- next_out: float32 [1024, 640], P(('ctx', 'fsdp'))
- next_out_first: float32 [1024, 640], P(('ctx', 'fsdp'))
- next_out_second: float32 [1024, 640], P(('ctx', 'fsdp'))
- next_gate_up: float32 [640, 4096], P(('ctx', 'fsdp'))
- next_gate_up_first: float32 [640, 4096], P(('ctx', 'fsdp'))
- next_gate_up_second: float32 [640, 4096], P(('ctx', 'fsdp'))
- next_down: float32 [2048, 640], P(('ctx', 'fsdp'))
- next_down_first: float32 [2048, 640], P(('ctx', 'fsdp'))
- next_down_second: float32 [2048, 640], P(('ctx', 'fsdp'))
- next_gains: float32 [2, 640], P(None, ('ctx', 'fsdp'))
- next_gains_first: float32 [2, 640], P(None, ('ctx', 'fsdp'))
- next_gains_second: float32 [2, 640], P(None, ('ctx', 'fsdp'))
All inputs are finite; a program needn't handle non-finite values.
Results may differ from a plain program's by a relative error of at most 0.034.
Values may be sent and summed in bfloat16 or wider, within the bound.
A program may use at most 128 MiB of HBM per device.

v0:
```python
import jax
import jax.numpy as jnp
from jax import lax
from jax.sharding import PartitionSpec as P

D = 640
HEADS = 4
HEAD = 256
FF = 2048
WINDOW = 512
STEP = 10
QW = 1024
OUT_FAN = 8


eps_norm = 1e-06
beta_one = 0.9
beta_two = 0.95
eps_adam = 1e-08
weight_decay = 0.1
masked_score = -1e30


def shifted(block, axis, distance):
    devices = range(lax.axis_size(axis))
    route = [(i - distance, i) for i in devices if i - distance in devices]
    return lax.ppermute(block, axis, route)


def normed(field, gain_row):
    return field * lax.rsqrt(jnp.mean(field * field, axis=-1, keepdims=True) + eps_norm) * gain_row


def rotated(field, cos_table, sin_table):
    half_width = field.shape[-1] // 2
    first_half = field[..., :half_width]
    second_half = field[..., half_width:]
    return jnp.concatenate(
        [
            first_half * cos_table - second_half * sin_table,
            second_half * cos_table + first_half * sin_table,
        ],
        axis=-1,
    )


def geglu(gate_part, up_part):
    return jax.nn.gelu(gate_part, approximate=True) * up_part


def adamw(master, first_state, second_state, gradient, rate, decay_rate):
    first_next = beta_one * first_state + (1.0 - beta_one) * gradient
    second_next = beta_two * second_state + (1.0 - beta_two) * gradient * gradient
    first_fixed = first_next / (1.0 - beta_one**STEP)
    second_fixed = second_next / (1.0 - beta_two**STEP)
    master_next = master - rate * (
        first_fixed / (jnp.sqrt(second_fixed) + eps_adam) + decay_rate * master
    )
    return (master_next, first_next, second_next)


def body(
    tokens,
    cotangent,
    starts,
    qkv_weight,
    qkv_first,
    qkv_second,
    out_weight,
    out_first,
    out_second,
    gate_up_weight,
    gate_up_first,
    gate_up_second,
    down_weight,
    down_first,
    down_second,
    norm_gains,
    gains_first,
    gains_second,
):
    length = tokens.shape[1]
    blocks = lax.axis_size("ctx")
    ctx_place = lax.axis_index("ctx")
    reach_back = min(blocks - 1, (WINDOW - 2) // length + 1)
    boundary = starts[0]
    row_places = ctx_place * length + jnp.arange(length, dtype=jnp.int32)
    half_width = HEAD // 2
    frequency = 10000.0 ** (-(2.0 * jnp.arange(half_width, dtype=jnp.float32)) / HEAD)
    angles = row_places.astype(jnp.float32)[:, None] * frequency[None, :]
    cos_table = jnp.cos(angles)
    sin_table = jnp.sin(angles)
    head_scale = HEAD ** (-0.5)
    qkv_matrix, out_matrix, gain_rows = (
        lax.all_gather(qkv_weight.astype(jnp.bfloat16), ("ctx", "fsdp"), axis=0, tiled=True),
        lax.all_gather(out_weight.astype(jnp.bfloat16), ("ctx", "fsdp"), axis=0, tiled=True),
        lax.all_gather(norm_gains.astype(jnp.bfloat16), ("ctx", "fsdp"), axis=1, tiled=True),
    )
    gate_up_matrix, down_matrix = (
        lax.all_gather(gate_up_weight.astype(jnp.bfloat16), ("ctx", "fsdp"), axis=0, tiled=True),
        lax.all_gather(down_weight.astype(jnp.bfloat16), ("ctx", "fsdp"), axis=0, tiled=True),
    )
    gain_first = gain_rows[0].astype(jnp.float32)
    gain_second = gain_rows[1].astype(jnp.float32)
    inputs = tokens[0].astype(jnp.float32)
    pulled = cotangent[0].astype(jnp.float32)
    first_normed = normed(inputs, gain_first).astype(jnp.bfloat16)
    projected = jnp.dot(first_normed, qkv_matrix, preferred_element_type=jnp.float32)
    queries = projected[:, :QW].reshape(length, HEADS, HEAD)
    queries = (rotated(queries, cos_table[:, None, :], sin_table[:, None, :]) * head_scale).astype(
        jnp.bfloat16
    )
    own_keys = rotated(projected[:, QW : QW + HEAD], cos_table, sin_table).astype(jnp.bfloat16)
    own_values = projected[:, QW + HEAD :].astype(jnp.bfloat16)
    key_parts = [own_keys]
    value_parts = [own_values]
    place_parts = [row_places]
    for back_step in range(1, reach_back + 1):
        came_keys, came_values = shifted((own_keys, own_values), "ctx", back_step)
        key_parts.append(came_keys)
        value_parts.append(came_values)
        place_parts.append(row_places - back_step * length)
    key_rows = jnp.concatenate(key_parts, axis=0)
    value_rows = jnp.concatenate(value_parts, axis=0)
    key_places = jnp.concatenate(place_parts, axis=0)
    query_document = row_places >= boundary
    key_document = key_places >= boundary
    distance = row_places[:, None] - key_places[None, :]
    allowed = (
        (distance >= 0)
        & (distance < WINDOW)
        & (key_places[None, :] >= 0)
        & (query_document[:, None] == key_document[None, :])
    )
    allowed = allowed[:, None, :]

    def masked_scores():
        raw_scores = jnp.einsum(
            "thd,kd->thk", queries, key_rows, preferred_element_type=jnp.float32
        )
        return jnp.where(allowed, raw_scores, masked_score)

    scores = masked_scores()
    row_max = jnp.max(scores, axis=-1, keepdims=True)
    exp_scores = jnp.exp(scores - row_max)
    exp_totals = jnp.sum(exp_scores, axis=-1, keepdims=True)
    soft_weights = exp_scores / exp_totals
    log_total = row_max + jnp.log(exp_totals)
    mixed_heads = jnp.einsum(
        "thk,kd->thd",
        soft_weights.astype(jnp.bfloat16),
        value_rows,
        preferred_element_type=jnp.float32,
    )
    mixed_heads = mixed_heads.reshape(length, QW).astype(jnp.bfloat16)
    first_out = inputs + jnp.dot(mixed_heads, out_matrix, preferred_element_type=jnp.float32)
    second_normed = normed(first_out, gain_second).astype(jnp.bfloat16)
    gate_up = jnp.dot(second_normed, gate_up_matrix, preferred_element_type=jnp.float32)
    gate_part = gate_up[:, :FF]
    up_part = gate_up[:, FF:]
    hidden = geglu(gate_part, up_part).astype(jnp.bfloat16)
    layer_out = first_out + jnp.dot(hidden, down_matrix, preferred_element_type=jnp.float32)
    pulled_low = cotangent[0]
    grad_down = jnp.einsum("tf,td->fd", hidden, pulled_low, preferred_element_type=jnp.float32)
    d_hidden = jnp.einsum("td,fd->tf", pulled_low, down_matrix, preferred_element_type=jnp.float32)
    geglu_pull = jax.vjp(geglu, gate_part, up_part)[1]
    d_gate, d_up = geglu_pull(d_hidden)
    d_gate_up = jnp.concatenate([d_gate, d_up], axis=1).astype(jnp.bfloat16)
    grad_gate_up = jnp.einsum(
        "td,tf->df", second_normed, d_gate_up, preferred_element_type=jnp.float32
    )
    d_second = jnp.einsum(
        "tf,df->td", d_gate_up, gate_up_matrix, preferred_element_type=jnp.float32
    )
    second_pull = jax.vjp(normed, first_out, gain_second)[1]
    d_residual, grad_gain_second = second_pull(d_second)
    d_first_out = pulled + d_residual
    d_attention = d_first_out.astype(jnp.bfloat16)
    grad_out = jnp.einsum("tq,td->qd", mixed_heads, d_attention, preferred_element_type=jnp.float32)
    d_mixed = jnp.einsum("td,qd->tq", d_attention, out_matrix, preferred_element_type=jnp.float32)
    d_mixed = d_mixed.astype(jnp.bfloat16).reshape(length, HEADS, HEAD)
    soft_again = jnp.exp(masked_scores() - log_total)
    d_soft = jnp.einsum("thd,kd->thk", d_mixed, value_rows, preferred_element_type=jnp.float32)
    grad_value_rows = jnp.einsum(
        "thk,thd->kd", soft_again.astype(jnp.bfloat16), d_mixed, preferred_element_type=jnp.float32
    )
    centered = jnp.sum(soft_again * d_soft, axis=-1, keepdims=True)
    d_scores = (soft_again * (d_soft - centered)).astype(jnp.bfloat16)
    d_queries = (
        jnp.einsum("thk,kd->thd", d_scores, key_rows, preferred_element_type=jnp.float32)
        * head_scale
    )
    grad_key_rows = jnp.einsum("thk,thd->kd", d_scores, queries, preferred_element_type=jnp.float32)
    d_keys = grad_key_rows[:length]
    d_values = grad_value_rows[:length]
    for back_step in range(1, reach_back + 1):
        lower_edge = back_step * length
        came_keys, came_values = (
            shifted(
                grad_key_rows[lower_edge : lower_edge + length].astype(jnp.bfloat16),
                "ctx",
                -back_step,
            ).astype(jnp.float32),
            shifted(
                grad_value_rows[lower_edge : lower_edge + length].astype(jnp.bfloat16),
                "ctx",
                -back_step,
            ).astype(jnp.float32),
        )
        d_keys = d_keys + came_keys
        d_values = d_values + came_values
    d_queries = rotated(d_queries, cos_table[:, None, :], -sin_table[:, None, :]).reshape(
        length, QW
    )
    d_keys = rotated(d_keys, cos_table, -sin_table)
    d_projected = jnp.concatenate([d_queries, d_keys, d_values], axis=1).astype(jnp.bfloat16)
    grad_qkv = jnp.einsum(
        "td,tc->dc", first_normed, d_projected, preferred_element_type=jnp.float32
    )
    d_first = jnp.einsum("tc,dc->td", d_projected, qkv_matrix, preferred_element_type=jnp.float32)
    first_pull = jax.vjp(normed, inputs, gain_first)[1]
    d_inputs, grad_gain_first = first_pull(d_first)
    input_grad = d_first_out + d_inputs
    grad_gains = jnp.stack([grad_gain_first, grad_gain_second], axis=0)
    share_qkv, share_out, share_gate_up, share_down, share_gains = (
        lax.psum_scatter(grad_qkv, ("ctx", "fsdp"), scatter_dimension=0, tiled=True),
        lax.psum_scatter(grad_out, ("ctx", "fsdp"), scatter_dimension=0, tiled=True),
        lax.psum_scatter(grad_gate_up, ("ctx", "fsdp"), scatter_dimension=0, tiled=True),
        lax.psum_scatter(grad_down, ("ctx", "fsdp"), scatter_dimension=0, tiled=True),
        lax.psum_scatter(grad_gains, ("ctx", "fsdp"), scatter_dimension=1, tiled=True),
    )
    qkv_new = adamw(qkv_weight, qkv_first, qkv_second, share_qkv, 1.5 * D ** (-0.5), weight_decay)
    out_new = adamw(
        out_weight, out_first, out_second, share_out, 1.5 * OUT_FAN ** (-0.5), weight_decay
    )
    gate_up_new = adamw(
        gate_up_weight,
        gate_up_first,
        gate_up_second,
        share_gate_up,
        1.5 * D ** (-0.5),
        weight_decay,
    )
    down_new = adamw(
        down_weight, down_first, down_second, share_down, 1.5 * FF ** (-0.5), weight_decay
    )
    gains_new = adamw(norm_gains, gains_first, gains_second, share_gains, 0.5, 0.0)
    return (
        layer_out[None],
        input_grad[None],
        qkv_new[0],
        qkv_new[1],
        qkv_new[2],
        out_new[0],
        out_new[1],
        out_new[2],
        gate_up_new[0],
        gate_up_new[1],
        gate_up_new[2],
        down_new[0],
        down_new[1],
        down_new[2],
        gains_new[0],
        gains_new[1],
        gains_new[2],
    )


def solution(mesh):
    return jax.shard_map(
        body,
        mesh=mesh,
        in_specs=(
            P("fsdp", "ctx", None),
            P("fsdp", "ctx", None),
            P("fsdp"),
            P(("ctx", "fsdp"), None),
            P(("ctx", "fsdp"), None),
            P(("ctx", "fsdp"), None),
            P(("ctx", "fsdp"), None),
            P(("ctx", "fsdp"), None),
            P(("ctx", "fsdp"), None),
            P(("ctx", "fsdp"), None),
            P(("ctx", "fsdp"), None),
            P(("ctx", "fsdp"), None),
            P(("ctx", "fsdp"), None),
            P(("ctx", "fsdp"), None),
            P(("ctx", "fsdp"), None),
            P(None, ("ctx", "fsdp")),
            P(None, ("ctx", "fsdp")),
            P(None, ("ctx", "fsdp")),
        ),
        out_specs=(
            P("fsdp", "ctx", None),
            P("fsdp", "ctx", None),
            P(("ctx", "fsdp"), None),
            P(("ctx", "fsdp"), None),
            P(("ctx", "fsdp"), None),
            P(("ctx", "fsdp"), None),
            P(("ctx", "fsdp"), None),
            P(("ctx", "fsdp"), None),
            P(("ctx", "fsdp"), None),
            P(("ctx", "fsdp"), None),
            P(("ctx", "fsdp"), None),
            P(("ctx", "fsdp"), None),
            P(("ctx", "fsdp"), None),
            P(("ctx", "fsdp"), None),
            P(None, ("ctx", "fsdp")),
            P(None, ("ctx", "fsdp")),
            P(None, ("ctx", "fsdp")),
        ),
        check_vma=False,
    )
```

profile of v0, /device:TPU:1, one launch (start us, length us, event | category | flops | bytes accessed | tf_op | source)
XLA Modules:
  0.0 1724.0 jit_solution(6073749133067793598)
XLA Ops:
  7.2 1.4 convert_bitcast_fusion.1
  8.7 1.3 convert_element_type.98
  10.1 1.5 convert_bitcast_fusion
  11.7 1.4 convert_element_type.102
  13.2 0.7 convert_bitcast_fusion.2
  14.5 179.3 %all-gather = bf16[128,5,2]{1,2,0:T(2,128)(2,1)S(1)} all-gather(bf16[1,5,2]{1,2,0:T(2,128)(2,1)S(1)} %convert_bitcast_fusion.2), channel_id=1, replica_groups=mesh['ctx'=8,'fsdp'=16] {'ctx','fsdp'}, dimensions={0}, use_global_device_ids=true | all-gather | bytes 2580 | tf_op jit(solution)/shard_map/all_gather | solution.py:97
  194.3 1.1 fusion.33
  195.4 1.0 fusion.25
  196.5 13.8 all-gather.12.cloned.1.call-done
  210.3 3.0 reshape.298
  213.3 0.8 fusion.66
  214.2 0.7 slice.148
  214.8 3.1 collective-permute-start.3
  218.0 3.4 collective-permute-start.2
  221.5 1.3 fusion.51
  222.8 0.7 pad_maximum_fusion.7
  223.5 1.9 collective-permute-start.1
  225.4 3.7 collective-permute-start
  229.8 1.0 multiply_subtract_fusion
  230.9 2.0 select_reduce_fusion
  233.0 0.8 fusion
  234.4 2.9 fusion.17
  237.4 167.0 %all-gather.8.cloned.1.call-done = bf16[1024,640]{1,0:T(8,128)(2,1)} async-done(((bf16[8,640]{1,0:T(8,128)(2,1)}), bf16[1024,640]{1,0:T(8,128)(2,1)}) %all-gather.8.cloned.1.call-update) | async-done | bytes 1310736 | tf_op jit(solution)/shard_map/all_gather | solution.py:96
  404.4 2.9 multiply_reduce_fusion.3
  407.9 199.8 %all-gather.14.cloned.1.call-done = bf16[128,5,4096]{2,1,0:T(8,128)(2,1)} async-done(((bf16[1,5,4096]{2,1,0:T(8,128)(2,1)}), bf16[128,5,4096]{2,1,0:T(8,128)(2,1)}) %all-gather.14.cloned.1.call-update) | async-done | bytes 5242896 | tf_op jit(solution)/shard_map/all_gather | solution.py:100
  607.7 8.8 reshape.300
  616.5 6.6 fusion.96
  623.0 181.7 %all-gather.10.cloned.1.call-done = bf16[2048,640]{1,0:T(8,128)(2,1)} async-done(((bf16[16,640]{1,0:T(8,128)(2,1)}), bf16[2048,640]{1,0:T(8,128)(2,1)}) %all-gather.10.cloned.1.call-update) | async-done | bytes 2621456 | tf_op jit(solution)/shard_map/all_gather | solution.py:101
  804.8 6.4 fusion.7
  811.2 2.5 multiply_reduce_fusion.1
  813.7 5.7 fusion.15
  819.7 0.8 copy-done.25
  820.4 2.1 fusion.47
  822.5 1.4 convolution_convert_fusion
  823.9 2.1 copy.87
  826.0 3.0 fusion.105
  829.0 0.7 fusion.104
  829.7 1.3 collective-permute-start.6
  831.0 1.5 collective-permute-start.7
  832.5 2.6 multiply_reduce_fusion
  835.2 0.8 multiply_convert_fusion
  836.3 1.5 fusion.106
  837.9 1.4 collective-permute-start.4
  839.3 1.3 collective-permute-start.5
  840.6 1.6 convolution_multiply_fusion
  842.7 1.7 collective-permute-done.4
  844.3 4.8 collective-permute-done.5
  849.1 1.0 fusion.41
  851.0 1.1 fusion.40
  852.8 2.7 fusion.54
  855.5 1.1 copy-done.7
  856.8 3.4 fusion.35
  861.2 3.9 fusion.21
  865.2 2.2 fusion.29
  867.5 64.8 %all-reduce.3 = f32[2,640]{1,0:T(2,128)S(1)} all-reduce(f32[2,640]{1,0:T(2,128)S(1)} %pad_maximum_fusion.8), channel_id=6, replica_groups=mesh['ctx'=8,'fsdp'=16] {'ctx','fsdp'}, use_global_device_ids=true, to_apply=%region_13.14.clone | all-reduce | flops 1280 | bytes 10240
  932.3 0.7 multiply_multiply_fusion.8
  933.0 1.4 multiply_subtract_fusion.5
  934.3 2.1 fusion.32
  936.5 140.1 %all-reduce.7.cloned.1.call-done = (f32[640,1536]{1,0:T(8,128)}, f32[1024,640]{1,0:T(8,128)}, f32[640,4096]{1,0:T(8,128)}) async-done(((f32[640,1536]{1,0:T(8,128)}, f32[1024,640]{1,0:T(8,128)}, f32[640,4096]{1,0:T(8,128)}), (f32[640,1536]{1,0:T(8,128)}, f32[1024,640]{1,0:T(8,128)}, f32[640,4096]{1,0:T(8,128)})) %all-reduce.7.cloned.1.call-update) | async-done | bytes 17039376
  1076.5 1.4 multiply_subtract_fusion.4
  1077.9 1.6 multiply_subtract_fusion.2
  1079.5 1.8 multiply_subtract_fusion.1
  1081.3 634.4 %reduce-scatter.3.cloned.1.call-done = f32[16,640]{1,0:T(8,128)} async-done(((f32[2048,640]{1,0:T(8,128)}), f32[16,640]{1,0:T(8,128)}) %reduce-scatter.3.cloned.1.call-update) | async-done | bytes 40976 | tf_op jit(solution)/shard_map/reduce_scatter | solution.py:229
  1715.8 1.4 multiply_subtract_fusion.3
  (148 shorter events, 6.3 us)
Async XLA Ops:
  7.2 203.1 %all-gather.12.cloned.1.call-start = ((), (), s32[]{:S(2)}) async-start(), calls=%async_computation.4 | async-start | bytes 3170304 | tf_op jit(solution)/shard_map/all_gather | solution.py:95
  8.7 395.7 %all-gather.8.cloned.1.call-start = ((), (), s32[]{:S(2)}) async-start(), calls=%async_computation.1 | async-start | bytes 1320960 | tf_op jit(solution)/shard_map/all_gather | solution.py:96
  10.1 597.6 %all-gather.14.cloned.1.call-start = ((), (), s32[]{:S(2)}) async-start(), calls=%async_computation.5 | async-start | bytes 8454144 | tf_op jit(solution)/shard_map/all_gather | solution.py:100
  11.7 793.1 %all-gather.10.cloned.1.call-start = ((), (), s32[]{:S(2)}) async-start(), calls=%async_computation.2 | async-start | bytes 2641920 | tf_op jit(solution)/shard_map/all_gather | solution.py:101
  13.1 1063.4 %all-reduce.7.cloned.1.call-start = ((), (), s32[]{:S(2)}) async-start(), calls=%async_computation.6 | async-start | bytes 34078720
  194.1 27.3 %copy-start.49 = (f32[128]{0:T(128)}, f32[128]{0:T(128)S(1)}, u32[]{:S(2)}) copy-start(f32[128]{0:T(128)S(1)} %multiply_power_fusion) | copy-start | bytes 1540
  194.2 27.3 %copy-start.44 = (f32[256]{0:T(256)}, f32[256]{0:T(256)S(1)}, u32[]{:S(2)}) copy-start(f32[256]{0:T(256)S(1)} %fusion.76) | copy-start | bytes 3076
  195.4 17.9 %copy-start.42 = (f32[256]{0:T(256)}, f32[256]{0:T(256)S(1)}, u32[]{:S(2)}) copy-start(f32[256]{0:T(256)S(1)} %fusion.33) | copy-start | bytes 3076
  195.4 17.9 %copy-start.36 = (f32[256]{0:T(256)}, f32[256]{0:T(256)S(1)}, u32[]{:S(2)}) copy-start(f32[256]{0:T(256)S(1)} %fusion.80) | copy-start | bytes 3076
  195.4 17.9 %copy-start.8 = (bf16[1,256,640]{2,1,0:T(8,128)(2,1)S(1)}, bf16[1,256,640]{2,1,0:T(8,128)(2,1)}, u32[]{:S(2)}) copy-start(bf16[1,256,640]{2,1,0:T(8,128)(2,1)} %param.18) | copy-start | bytes 983044
  213.3 8.2 copy-start.5
  214.8 19.0 %collective-permute-start.3 = (bf16[256,256]{1,0:T(8,128)(2,1)}, bf16[256,256]{1,0:T(8,128)(2,1)}, u32[]{:S(2)}, u32[]{:S(2)}) collective-permute-start(bf16[256,256]{1,0:T(8,128)(2,1)} %slice.148), channel_id=1, source_target_pairs={{0,32},{16,48},{32,64},{48,80},{64,96},{80,112},{1,33},{17,49},{33... | collective-permute-start | bytes 393224 | tf_op jit(solution)/shard_map/ppermute | solution.py:27
  218.0 15.9 collective-permute-start.2
  222.8 2.7 copy-start.28
  222.8 8.1 copy-start.15
  223.5 7.4 collective-permute-start.1
  225.4 5.5 collective-permute-start
  229.6 1.3 copy-start.9
  229.6 1.3 copy-start.29
  230.9 2.1 copy-start.21
  230.9 2.1 copy-start.23
  233.0 0.9 copy-start.38
  404.4 3.5 copy-start.39
  404.4 3.5 copy-start.41
  804.8 6.4 copy-start
  804.8 6.4 copy-start.1
  813.7 5.7 copy-start.47
  813.7 5.7 copy-start.12
  819.4 1.0 copy-start.25
  819.4 3.1 copy-start.14
  820.4 2.1 copy-start.3
  826.0 6.6 copy-start.10
  826.0 6.6 copy-start.11
  829.7 21.3 %collective-permute-start.6 = (bf16[256,256]{0,1:T(8,128)(2,1)}, bf16[256,256]{0,1:T(8,128)(2,1)}, u32[]{:S(2)}, u32[]{:S(2)}) collective-permute-start(bf16[256,256]{0,1:T(8,128)(2,1)} %get-tuple-element.54), channel_id=1, source_target_pairs={{16,0},{32,16},{48,32},{64,48},{80,64},{96,80},{112,96},{17,1},{33... | collective-permute-start | bytes 393224 | tf_op jit(solution)/shard_map/ppermute | solution.py:27
  831.0 20.0 %collective-permute-start.7 = (bf16[256,256]{0,1:T(8,128)(2,1)}, bf16[256,256]{0,1:T(8,128)(2,1)}, u32[]{:S(2)}, u32[]{:S(2)}) collective-permute-start(bf16[256,256]{0,1:T(8,128)(2,1)} %get-tuple-element.55), channel_id=1, source_target_pairs={{32,0},{48,16},{64,32},{80,48},{96,64},{112,80},{33,1},{49,17},{65... | collective-permute-start | bytes 393224 | tf_op jit(solution)/shard_map/ppermute | solution.py:27
  835.1 1.0 copy-start.22
  835.2 1.2 copy-start.24
  836.3 4.3 copy-start.30
  837.8 4.4 copy-start.16
  837.8 4.4 copy-start.17
  837.9 6.5 collective-permute-start.4
  839.3 9.8 collective-permute-start.5
  842.2 8.0 copy-start.45
  842.2 8.0 copy-start.50
  842.2 10.5 copy-start.37
  851.0 4.5 copy-start.26
  852.1 0.7 copy-start.18
  855.5 1.2 copy-start.7
  855.5 1.3 copy-start.13
  855.5 860.3 %reduce-scatter.3.cloned.1.call-start = ((), (), s32[]{:S(2)}) async-start(), calls=%async_computation.3 | async-start | bytes 5283840 | tf_op jit(solution)/shard_map/reduce_scatter | solution.py:229
  860.1 0.7 copy-start.48
  860.1 1.1 copy-start.2
  860.2 5.0 copy-start.6
  860.2 4.9 copy-start.19
  860.2 4.9 copy-start.27
  865.1 67.1 %copy-start.43 = (f32[256]{0:T(256)S(1)}, f32[256]{0:T(256)}, u32[]{:S(2)}) copy-start(f32[256]{0:T(256)} %copy-done.42) | copy-start | bytes 3076
  865.1 67.8 %copy-start.51 = (f32[2,5]{1,0:T(2,128)S(1)}, f32[2,5]{1,0:T(2,128)}, u32[]{:S(2)}) copy-start(f32[2,5]{1,0:T(2,128)} %param.33) | copy-start | bytes 124
  865.1 69.2 %copy-start.4 = (f32[256,640]{1,0:T(8,128)S(1)}, f32[256,640]{1,0:T(8,128)}, u32[]{:S(2)}) copy-start(f32[256,640]{1,0:T(8,128)} %copy-done.3) | copy-start | bytes 1966084
  867.4 212.1 %copy-start.20 = (f32[5,4096]{1,0:T(8,128)S(1)}, f32[5,4096]{1,0:T(8,128)}, u32[]{:S(2)}) copy-start(f32[5,4096]{1,0:T(8,128)} %param.27) | copy-start | bytes 245764
  867.4 212.1 %copy-start.32 = (f32[5,4096]{1,0:T(8,128)S(1)}, f32[5,4096]{1,0:T(8,128)}, u32[]{:S(2)}) copy-start(f32[5,4096]{1,0:T(8,128)} %param.28) | copy-start | bytes 245764
  867.4 212.1 %copy-start.33 = (f32[5,4096]{1,0:T(8,128)S(1)}, f32[5,4096]{1,0:T(8,128)}, u32[]{:S(2)}) copy-start(f32[5,4096]{1,0:T(8,128)} %param.29) | copy-start | bytes 245764
  867.4 848.3 %copy-start.31 = (f32[16,640]{1,0:T(8,128)S(1)}, f32[16,640]{1,0:T(8,128)}, u32[]{:S(2)}) copy-start(f32[16,640]{1,0:T(8,128)} %param.30) | copy-start | bytes 122884
  867.4 848.3 %copy-start.34 = (f32[16,640]{1,0:T(8,128)S(1)}, f32[16,640]{1,0:T(8,128)}, u32[]{:S(2)}) copy-start(f32[16,640]{1,0:T(8,128)} %param.31) | copy-start | bytes 122884
  867.4 848.3 %copy-start.35 = (f32[16,640]{1,0:T(8,128)S(1)}, f32[16,640]{1,0:T(8,128)}, u32[]{:S(2)}) copy-start(f32[16,640]{1,0:T(8,128)} %param.32) | copy-start | bytes 122884
  (2 other events, 1.2 us)
Sparse Core Ops, SparseCore 0:
  10.3 199.9 all-gather.11
  212.6 191.7 all-gather.7
  406.1 201.5 all-gather.13
  609.9 194.8 all-gather.9
  855.6 220.8 all-reduce.6
  1078.9 636.8 reduce-scatter.2
where the time goes:
time: 1730 us; the launch traced here: 1720 us
  waiting for transfers between devices  1340 us (77%)
  blocking collectives  244 us (14%)
  matrix products  54.3 us (3%)
  other arithmetic  26.8 us (2%)
  local copies, waits for them, and re-layouts  21.9 us (1%)
  starting transfers between devices  17.9 us (1%)
    reduce_scatter x1, waiting for transfers between devices, body(): lax.psum_scatter(grad_down, ('ctx', 'fsdp'), scatter_dimension=0, tiled=T...  634 us
    all_gather x1, waiting for transfers between devices, body(): lax.all_gather(gate_up_weight.astype(jnp.bfloat16), ('ctx', 'fsdp'), axis...  200 us
    all_gather x1, waiting for transfers between devices, body(): lax.all_gather(down_weight.astype(jnp.bfloat16), ('ctx', 'fsdp'), axis=0,...  182 us
    all_gather x1, blocking collectives, body(): lax.all_gather(norm_gains.astype(jnp.bfloat16), ('ctx', 'fsdp'), axis=1,...  179 us
    all_gather x1, waiting for transfers between devices, body(): lax.all_gather(out_weight.astype(jnp.bfloat16), ('ctx', 'fsdp'), axis=0,...  167 us
    unnamed x7, waiting for transfers between devices  140 us
    unnamed x1, blocking collectives  64.8 us
  transfers between devices with their start and end apart: 14, of which 8 were waited for; matrix products, arithmetic and copies ran while one was open for 4% of the time, Pallas kernels for 0%

commit v1 on v0

v1 whole, which is shorter than its diff:
```python
import functools

import jax
import jax.numpy as jnp
import numpy as np
from jax import lax
from jax.experimental import pallas as pl
from jax.experimental.pallas import tpu as pltpu
from jax.sharding import PartitionSpec as P

D = 640
HEADS = 4
HEAD = 256
FF = 2048
WINDOW = 512
STEP = 10
QW = 1024
OUT_FAN = 8
TOK = 256
LENGTH = 2048

eps_norm = 1e-06
beta_one = 0.9
beta_two = 0.95
eps_adam = 1e-08
weight_decay = 0.1
masked_score = -1e30

MESH = pl.DeviceIdType.MESH
BF = jnp.bfloat16
F32 = jnp.float32


class Place:
    def __init__(self):
        self.ctx = lax.axis_index("ctx")
        self.fsdp = lax.axis_index("fsdp")
        self.x = lax.div(self.ctx, 2)
        self.zl = lax.rem(self.ctx, 2)
        self.zh = lax.div(self.fsdp, 8)
        self.y = lax.div(lax.rem(self.fsdp, 8), 2)
        self.k = lax.rem(self.fsdp, 2)
        self.z = 2 * self.zh + self.zl


def device(x, y, z, k):
    return (2 * x + lax.rem(z, 2), 8 * lax.div(z, 2) + 2 * y + k)


def around(a, b):
    return lax.rem(a + b, 4)


def plane_chip(me, last, j):
    a, b = lax.rem(j, 4), lax.div(j, 4)
    if last == XA:
        return me.x, around(me.y, a), around(me.z, b)
    if last == YA:
        return around(me.x, a), me.y, around(me.z, b)
    return around(me.x, a), around(me.y, b), me.z


def line_chip(me, last, j):
    if last == XA:
        return around(me.x, j), me.y, me.z
    if last == YA:
        return me.x, around(me.y, j), me.z
    return me.x, me.y, around(me.z, j)


def along(me, last):
    return (me.x, me.y, me.z)[last]


def in_plane(last, x, y, z):
    if last == XA:
        return lax.rem(z, 2) * 8 + lax.div(z, 2) * 4 + y
    if last == YA:
        return 4 * x + z
    return 4 * x + y


def rows(start, size):
    return pl.ds(pl.multiple_of(start, 16), size)


def feature_order(last):
    order = np.zeros(D, np.int64)
    for x in range(4):
        for y in range(4):
            for z in range(4):
                for k in range(2):
                    dev = x * 32 + (z % 2) * 16 + (z // 2) * 8 + y * 2 + k
                    b, p = (y, 4 * x + z) if last == YA else (z, 4 * x + y)
                    for r in range(5):
                        order[b * 160 + k * 80 + p * 5 + r] = 5 * dev + r
    return order


def constants():
    orders = np.zeros((2, D, D), np.float32)
    for n, last in enumerate((YA, ZA)):
        orders[n, feature_order(last), np.arange(D)] = 1.0
    pick5 = np.zeros((3, 160, 512), np.float32)
    for g in range(3):
        for s in range(32):
            for r in range(5):
                pick5[g, s * 5 + r, s * 16 + g * 5 + r] = 1.0
    pick8 = np.zeros((2, 128, 256), np.float32)
    for g in range(2):
        for s in range(16):
            for r in range(8):
                pick8[g, s * 8 + r, s * 16 + g * 8 + r] = 1.0
    half = HEAD // 2
    frequency = np.float32(10000.0) ** (
        -(np.float32(2.0) * np.arange(half, dtype=np.float32)) / np.float32(HEAD)
    )
    angles = np.arange(LENGTH, dtype=np.float32)[:, None] * frequency.astype(np.float32)[None, :]
    rope = np.stack([np.cos(angles.astype(np.float64)), np.sin(angles.astype(np.float64))])
    return (
        jnp.asarray(orders, BF),
        jnp.asarray(pick5, BF),
        jnp.asarray(pick8, BF),
        jnp.asarray(rope.astype(np.float32)),
    )


def dot(a, b):
    return lax.dot_general(a, b, (((1,), (0,)), ((), ())), preferred_element_type=F32)


def dot_nt(a, b):
    return lax.dot_general(a, b, (((1,), (1,)), ((), ())), preferred_element_type=F32)


def dot_tn(a, b):
    return lax.dot_general(a, b, (((0,), (0,)), ((), ())), preferred_element_type=F32)


def rotate(u, cos, sin):
    a, b = u[:, :128], u[:, 128:]
    return jnp.concatenate([a * cos - b * sin, b * cos + a * sin], axis=1)


def column(row):
    n = row.shape[1]
    i = lax.broadcasted_iota(jnp.int32, (n, n), 0)
    j = lax.broadcasted_iota(jnp.int32, (n, n), 1)
    wide = jnp.broadcast_to(row.astype(BF).astype(F32), (n, n))
    return jnp.sum(jnp.where(i == j, wide, 0.0), axis=1, keepdims=True)


class Bag(dict):
    __getattr__ = dict.__getitem__


def scratch_list():
    def v(*shape, kind=BF):
        return pltpu.VMEM(shape, kind)

    qkv = [
        Bag(
            pk=v(16, 256),
            st=v(256, 256),
            w=v(640, 512),
            g=v(640, 512),
            r0=v(320, 512),
            gs=v(320, 512),
            r1=v(240, 512),
            gp=v(256, 256),
            r2=v(256, 256),
        )
        for n in range(3)
    ]
    out = Bag(
        pk=v(16, 384),
        st=v(256, 384),
        w=v(1024, 640),
        g=v(1024, 640),
        r0=v(512, 640),
        gs=v(512, 640),
        r1=v(384, 640),
        gp=v(256, 384),
        r2=v(256, 384),
    )
    gate_up = [
        Bag(
            pk=v(32, 384),
            st=v(512, 384),
            w=v(640, 1024),
            g=v(640, 1024),
            r1=v(480, 1024),
            gp=v(512, 384),
            r2=v(512, 384),
        )
        for n in range(2)
    ]
    down = Bag(
        pk=v(16, 640),
        w=v(1024, 640),
        g=v(1024, 640),
        r1=v(768, 640),
        gp=v(256, 640),
        r2=v(256, 640),
    )
    return Bag(
        part=qkv + [out] + gate_up + [down],
        xin=v(TOK, D),
        cin=v(TOK, D),
        orders=v(2, D, D),
        pick5=v(3, 160, 512),
        pick8=v(2, 128, 256),
        rope=v(2, TOK, 128, kind=F32),
        pad=v(16, 384, kind=F32),
        xn=v(3, TOK, D),
        qs=v(HEADS * TOK, HEAD),
        kv=v(3 * TOK, 2 * HEAD),
        bias=v(TOK, 3 * TOK, kind=F32),
        probs=v(HEADS * TOK, 3 * TOK),
        ds=v(HEADS * TOK, 3 * TOK),
        mixed=v(TOK, QW),
        dmix=v(HEADS * TOK, HEAD),
        x1=v(TOK, D, kind=F32),
        x2=v(2 * TOK, D),
        x2z=v(2 * TOK, D),
        dy2=v(2 * TOK, D),
        outp=v(2 * TOK, D, kind=F32),
        ex=v(2 * TOK, D, kind=F32),
        ez=v(2 * TOK, D, kind=F32),
        osend=v(TOK, D),
        orecv=v(TOK, D),
        esend=v(TOK, D),
        erecv=v(TOK, D),
        dx1=v(TOK, D, kind=F32),
        dq=v(TOK, 1536),
        dkv=v(TOK, 2 * HEAD, kind=F32),
        kvsend=v(2 * TOK, 2 * HEAD),
        kvrecv=v(2 * TOK, 2 * HEAD),
    )


def leaves(tree):
    if isinstance(tree, dict):
        return [leaf for branch in tree.values() for leaf in leaves(branch)]
    if isinstance(tree, list):
        return [leaf for branch in tree for leaf in leaves(branch)]
    return [tree]


def refill(tree, values):
    if isinstance(tree, dict):
        return Bag({key: refill(branch, values) for key, branch in tree.items()})
    if isinstance(tree, list):
        return [refill(branch, values) for branch in tree]
    return next(values)


OUT, GATE, UP, DOWN = 3, 4, 5, 6
A, B, C, DD, E, FR = range(6)
DY, X2, EE, OO, KV, DKV = range(7, 13)
XA, YA, ZA = range(3)
LAST = (XA, YA, ZA, XA, XA, ZA, YA)


SEMS = 64


def wait_for(ref, sem):
    pltpu.make_async_copy(ref, ref, sem).wait()


def step_kernel(shape, *refs):
    (tok, cot, starts, wq, wo, wgu, wd, gains, orders_h, pick5_h, pick8_h, rope_h) = refs[:12]
    (lo, ig, sq0, sq1, sq2, so, sg, su, sd) = refs[12:21]
    s = refill(shape, iter(refs[21:-3]))
    local, sent, came = refs[-3:]
    me = Place()
    sems = {}

    def sem_of(name):
        return sems.setdefault(name, len(sems))

    def remote(src, dst, name, target):
        n = sem_of(name)
        pltpu.make_async_remote_copy(
            src_ref=src,
            dst_ref=dst,
            send_sem=sent.at[n],
            recv_sem=came.at[n],
            device_id=target,
            device_id_type=MESH,
        ).start()

    def own_copy(src, dst, name):
        pltpu.make_async_copy(src, dst, came.at[sem_of(name)]).start()

    def arrived(ref, name):
        wait_for(ref, came.at[sem_of(name)])

    def left(ref, name):
        wait_for(ref, sent.at[sem_of(name)])

    sibling = device(me.x, me.y, me.z, 1 - me.k)

    fetch = [
        (tok.at[0], s.xin),
        (orders_h, s.orders),
        (pick5_h, s.pick5),
        (pick8_h, s.pick8),
        (rope_h.at[:, pl.ds(pl.multiple_of(me.ctx * TOK, TOK), TOK), :], s.rope),
        (cot.at[0], s.cin),
        (cot.at[0], s.dy2.at[pl.ds(0, TOK)]),
    ]
    fetches = [pltpu.make_async_copy(a, b, local.at[n]) for n, (a, b) in enumerate(fetch)]
    for one in fetches:
        one.start()

    barrier = pltpu.get_barrier_semaphore()

    def greet(j, carry):
        for last in range(3):
            chip = plane_chip(me, last, j)
            for core in range(2):
                pl.semaphore_signal(barrier, inc=1, device_id=device(*chip, core), device_id_type=MESH)
        return carry

    lax.fori_loop(1, 16, greet, 0)
    pl.semaphore_signal(barrier, inc=1, device_id=sibling, device_id_type=MESH)

    pad = s.pad
    pad[...] = jnp.zeros((16, 384), F32)
    wqb = wq[...].astype(BF).astype(F32) * column(gains[0:1, :])
    for n in range(3):
        for g in range(2):
            pad[5 * g : 5 * g + 5, 0:256] = wqb[:, n * 512 + g * 256 : n * 512 + g * 256 + 256]
        s.part[n].pk[...] = pad[:, 0:256].astype(BF)
    gain = column(gains[1:2, :])
    for n, name in enumerate((GATE, UP)):
        for c in range(2):
            for t in range(8):
                g, i = t // 3, t % 3
                base = n * FF + (t // 2) * 512 + c * 256 + (t % 2) * 128
                pad[5 * g : 5 * g + 5, i * 128 : i * 128 + 128] = (
                    wgu[:, base : base + 128].astype(BF).astype(F32) * gain
                )
            pad[10:15, 256:384] = jnp.zeros((5, 128), F32)
            s.part[name].pk[c * 16 : c * 16 + 16, :] = pad[...].astype(BF)
    pad[0:8, :] = wo[:, 0:384]
    pad[8:16, 0:256] = wo[:, 384:640]
    pad[8:16, 256:384] = jnp.zeros((8, 128), F32)
    s.part[OUT].pk[...] = pad[...].astype(BF)
    s.part[DOWN].pk[...] = wd[...].astype(BF)

    pl.semaphore_wait(barrier, 91)

    def spread_same(last, src, dst, name):
        slot = in_plane(last, me.x, me.y, me.z)
        place = dst.at[rows(slot * 16, 16)]
        own_copy(src, place, name)

        def send(j, carry):
            remote(src, place, name, device(*plane_chip(me, last, j), me.k))
            return carry

        lax.fori_loop(1, 16, send, 0)

    def spread_low(last, src, place, name):
        def send(j, carry):
            remote(src, place, name, device(*plane_chip(me, last, j), me.zl))
            return carry

        lax.fori_loop(1, 16, send, 0)

        @pl.when(me.zl == me.k)
        def _():
            own_copy(src, place, name)

        @pl.when(me.zl != me.k)
        def _():
            remote(src, place, name, sibling)

    def spread_both(last, src, slot, dst, name):
        place = dst.at[rows(slot * 16, 16)]

        def send(j, carry):
            for core in range(2):
                remote(
                    src.at[pl.ds(core * 16, 16)],
                    place,
                    name,
                    device(*plane_chip(me, last, j), core),
                )
            return carry

        lax.fori_loop(1, 16, send, 0)
        own_copy(src.at[rows(me.k * 16, 16)], place, name)
        remote(src.at[rows((1 - me.k) * 16, 16)], place, name, sibling)

    low_slot = (me.zh * 4 + me.y) * 2 + me.k
    spread_same(ZA, s.part[2].pk, s.part[2].st, (2, A))
    spread_same(YA, s.part[1].pk, s.part[1].st, (1, A))
    spread_low(XA, s.part[0].pk, s.part[0].st.at[rows(low_slot * 16, 16)], (0, A))

    fetches[0].wait()
    fetches[1].wait()
    x = s.xin[...].astype(F32)
    r0 = lax.rsqrt(jnp.mean(x * x, axis=1, keepdims=True) + eps_norm)
    xn = (x * r0).astype(BF)
    s.xn[0] = xn
    s.xn[1] = dot(xn, s.orders[0]).astype(BF)
    s.xn[2] = dot(xn, s.orders[1]).astype(BF)
    for n in range(2, len(fetches)):
        fetches[n].wait()
    remote(s.cin, s.dy2.at[pl.ds(TOK, TOK)], DY, sibling)

    def pass_on(last, ref, name, place, size):
        for j in range(1, 4):
            remote(
                ref.at[rows(place, size)],
                ref.at[rows(place, size)],
                name,
                device(*line_chip(me, last, j), me.k),
            )

    for n in (2, 1, 0):
        last = LAST[n]
        arrived(s.part[n].st, (n, A))
        place = along(me, last) * 160 + me.k * 80
        st = s.part[n].st[...]
        w = s.part[n].w
        for g in range(2):
            w[rows(place, 80), g * 256 : g * 256 + 256] = dot(
                s.pick5[g, 0:80, 0:256], st
            ).astype(BF)
        pass_on(last, w, (n, B), place, 80)

    spread_low(XA, s.part[OUT].pk, s.part[OUT].st.at[rows(low_slot * 16, 16)], (OUT, A))
    spread_both(XA, s.part[GATE].pk, in_plane(XA, me.x, me.y, me.z) * 2 + me.k, s.part[GATE].st, (GATE, A))
    spread_both(ZA, s.part[UP].pk, me.k * 16 + in_plane(ZA, me.x, me.y, me.z), s.part[UP].st, (UP, A))
    down_row = me.x * 256 + me.zh * 128 + me.y * 32 + me.k * 16
    spread_low(YA, s.part[DOWN].pk, s.part[DOWN].w.at[rows(down_row, 16)], (DOWN, A))

    def to_sibling(ref, name, size, place):
        for b in range(4):
            remote(
                ref.at[rows(b * 2 * size + place, size)],
                ref.at[rows(b * 2 * size + place, size)],
                name,
                sibling,
            )

    for n in (2, 1, 0):
        arrived(s.part[n].w.at[pl.ds(0, 240)], (n, B))
        to_sibling(s.part[n].w, (n, C), 80, me.k * 80)

    kv = s.kv
    cos = s.rope[0]
    sin = s.rope[1]
    arrived(s.part[2].w.at[pl.ds(0, 320)], (2, C))
    own = dot(s.xn[2], s.part[2].w[...])
    kv[0:TOK, 0:HEAD] = rotate(own[:, 0:HEAD], cos, sin).astype(BF)
    kv[0:TOK, HEAD:] = own[:, HEAD:].astype(BF)
    for back in (1, 2):

        @pl.when(me.ctx + back < 8)
        def _():
            remote(
                kv.at[pl.ds(0, TOK)],
                kv.at[pl.ds(back * TOK, TOK)],
                (KV, back),
                (me.ctx + back, me.fsdp),
            )

        @pl.when(me.ctx < back)
        def _():
            kv[back * TOK : back * TOK + TOK, :] = jnp.zeros((TOK, 2 * HEAD), BF)

    for n in (1, 0):
        arrived(s.part[n].w.at[pl.ds(0, 320)], (n, C))
        part = dot(s.xn[n], s.part[n].w[...])
        for i in range(2):
            h = 2 * n + i
            s.qs[h * TOK : h * TOK + TOK, :] = (
                rotate(part[:, i * HEAD : i * HEAD + HEAD], cos, sin) * HEAD**-0.5
            ).astype(BF)

    boundary = starts[0]
    qi = lax.broadcasted_iota(jnp.int32, (TOK, TOK), 0)
    kj = lax.broadcasted_iota(jnp.int32, (TOK, TOK), 1)
    query_place = me.ctx * TOK + qi
    query_doc = (query_place >= boundary).astype(jnp.int32)
    for back in range(3):
        key_place = (me.ctx - back) * TOK + kj
        gap = query_place - key_place
        key_doc = (key_place >= boundary).astype(jnp.int32)
        allowed = (gap >= 0) & (gap < WINDOW) & (key_place >= 0) & (query_doc == key_doc)
        s.bias[:, back * TOK : back * TOK + TOK] = jnp.where(allowed, 0.0, masked_score)

    def unpack5(name, last):
        arrived(s.part[name].st, (name, A))
        place = along(me, last) * 160
        st = s.part[name].st[...]
        for g in range(3):
            width = 384 if g < 2 else 256
            s.part[name].w[rows(place, 160), g * 384 : g * 384 + width] = dot(
                s.pick5[g], st[:, 0:width]
            ).astype(BF)
        pass_on(last, s.part[name].w, (name, B), place, 160)

    arrived(s.part[OUT].st, (OUT, A))
    st = s.part[OUT].st[...]
    place = me.x * 256 + me.k * 128
    s.part[OUT].w[rows(place, 128), 0:384] = dot(s.pick8[0], st).astype(BF)
    s.part[OUT].w[rows(place, 128), 384:640] = dot(s.pick8[1], st[:, 0:256]).astype(BF)
    pass_on(XA, s.part[OUT].w, (OUT, B), place, 128)
    unpack5(GATE, XA)
    unpack5(UP, ZA)
    arrived(s.part[DOWN].w.at[pl.ds(0, 256)], (DOWN, A))
    for piece in range(8):
        pass_on(YA, s.part[DOWN].w, (DOWN, B), piece * 128 + me.y * 32, 32)

    for back in (1, 2):

        @pl.when(me.ctx >= back)
        def _():
            arrived(kv.at[pl.ds(back * TOK, TOK)], (KV, back))

    def head_forward(h, carry):
        hs = pl.ds(pl.multiple_of(h * TOK, TOK), TOK)
        scores = dot_nt(s.qs[hs, :], kv[:, 0:HEAD]) + s.bias[...]
        top = jnp.max(scores, axis=1, keepdims=True)
        e = jnp.exp(scores - top)
        p = (e * (1.0 / jnp.sum(e, axis=1, keepdims=True))).astype(BF)
        s.probs[hs, :] = p
        s.mixed[:, hs] = dot(p, kv[:, HEAD:]).astype(BF)
        return carry

    lax.fori_loop(0, HEADS, head_forward, 0)

    arrived(s.part[OUT].w.at[pl.ds(0, 384)], (OUT, B))
    to_sibling(s.part[OUT].w, (OUT, C), 128, me.k * 128)
    arrived(s.part[OUT].w.at[pl.ds(0, 512)], (OUT, C))
    x1 = x + dot(s.mixed[...], s.part[OUT].w[...])
    s.x1[...] = x1
    r1 = lax.rsqrt(jnp.mean(x1 * x1, axis=1, keepdims=True) + eps_norm)
    s.x2[0:TOK, :] = (x1 * r1).astype(BF)
    remote(s.x2.at[pl.ds(0, TOK)], s.x2.at[pl.ds(TOK, TOK)], X2, sibling)
    arrived(s.dy2.at[pl.ds(TOK, TOK)], DY)
    s.outp[...] = jnp.zeros((2 * TOK, D), F32)
    s.ex[...] = jnp.zeros((2 * TOK, D), F32)
    s.ez[...] = jnp.zeros((2 * TOK, D), F32)
    s.x2z[0:TOK, :] = dot(s.x2[0:TOK, :], s.orders[1]).astype(BF)
    arrived(s.x2.at[pl.ds(TOK, TOK)], X2)
    s.x2z[TOK:, :] = dot(s.x2[TOK:, :], s.orders[1]).astype(BF)
    arrived(s.part[GATE].w.at[pl.ds(0, 480)], (GATE, B))
    arrived(s.part[UP].w.at[pl.ds(0, 480)], (UP, B))
    arrived(s.part[DOWN].w.at[pl.ds(0, 768)], (DOWN, B))

    root = 0.7978845608028654

    def hidden_step(t, carry):
        ts = pl.ds(pl.multiple_of(t * 256, 256), 256)
        gate = dot(s.x2[...], s.part[GATE].w[:, ts])
        up = dot(s.x2z[...], s.part[UP].w[:, ts])
        d_hidden = dot_nt(s.dy2[...], s.part[DOWN].w[ts, :])
        square = gate * gate
        th = jnp.tanh(root * gate * (1.0 + 0.044715 * square))
        half = 0.5 * (1.0 + th)
        act = gate * half
        slope = half + 0.5 * gate * (1.0 - th * th) * (root * (1.0 + 0.134145 * square))
        hidden = (act * up).astype(BF)
        d_gate = (d_hidden * up * slope).astype(BF)
        d_up = (d_hidden * act).astype(BF)
        s.part[DOWN].g[ts, :] = dot_tn(hidden, s.dy2[...]).astype(BF)
        s.outp[...] += dot(hidden, s.part[DOWN].w[ts, :])
        s.part[GATE].g[:, ts] = dot_tn(s.x2[...], d_gate).astype(BF)
        s.ex[...] += dot_nt(d_gate, s.part[GATE].w[:, ts])
        s.part[UP].g[:, ts] = dot_tn(s.x2z[...], d_up).astype(BF)
        s.ez[...] += dot_nt(d_up, s.part[UP].w[:, ts])
        return carry

    lax.fori_loop(0, 4, hidden_step, 0)

    def gather_line(last, src, size, name):
        for j in range(1, 4):
            b = around(along(me, last), j)
            remote(
                src.at[rows(b * size, size)],
                s.part[name].r1.at[pl.ds((j - 1) * size, size)],
                (name, E),
                device(*line_chip(me, last, j), me.k),
            )

    other = s.ex[TOK:, :] + dot_nt(s.ez[TOK:, :].astype(BF), s.orders[1])
    s.esend[...] = other.astype(BF)
    remote(s.esend, s.erecv, EE, sibling)
    s.osend[...] = s.outp[TOK:, :].astype(BF)
    remote(s.osend, s.orecv, OO, sibling)

    for j in range(1, 4):
        b = around(me.y, j)
        for piece in range(8):
            remote(
                s.part[DOWN].g.at[rows(piece * 128 + b * 32, 32)],
                s.part[DOWN].r1.at[pl.ds((j - 1) * 256 + piece * 32, 32)],
                (DOWN, E),
                device(*line_chip(me, YA, j), me.k),
            )
    gather_line(XA, s.part[GATE].g, 160, GATE)
    gather_line(ZA, s.part[UP].g, 160, UP)

    e1 = s.ex[0:TOK, :] + dot_nt(s.ez[0:TOK, :].astype(BF), s.orders[1])
    arrived(s.erecv, EE)
    e1 = e1 + s.erecv[...].astype(F32)
    x1 = s.x1[...]
    r1 = lax.rsqrt(jnp.mean(x1 * x1, axis=1, keepdims=True) + eps_norm)
    dx1 = (
        s.cin[...].astype(F32)
        + r1 * e1
        - x1 * (r1 * r1 * r1 * jnp.mean(x1 * e1, axis=1, keepdims=True))
    )
    s.dx1[...] = dx1
    da = dx1.astype(BF)

    def head_out(h, carry):
        hs = pl.ds(pl.multiple_of(h * TOK, TOK), TOK)
        dmix = dot_nt(da, s.part[OUT].w[hs, :]).astype(BF)
        s.dmix[hs, :] = dmix
        d_probs = dot_nt(dmix, kv[:, HEAD:])
        p = s.probs[hs, :].astype(F32)
        center = jnp.sum(p * d_probs, axis=1, keepdims=True)
        s.ds[hs, :] = (p * (d_probs - center)).astype(BF)
        return carry

    lax.fori_loop(0, HEADS, head_out, 0)

    for back in (2, 1):
        bs = slice(back * TOK, back * TOK + TOK)
        to = slice((back - 1) * TOK, back * TOK)
        s.kvsend[to, 0:HEAD] = dot_tn(s.ds[:, bs], s.qs[...]).astype(BF)
        s.kvsend[to, HEAD:] = dot_tn(s.probs[:, bs], s.dmix[...]).astype(BF)

        @pl.when(me.ctx >= back)
        def _():
            remote(
                s.kvsend.at[pl.ds((back - 1) * TOK, TOK)],
                s.kvrecv.at[pl.ds((back - 1) * TOK, TOK)],
                (DKV, back),
                (me.ctx - back, me.fsdp),
            )

        @pl.when(me.ctx + back >= 8)
        def _():
            s.kvrecv[to, :] = jnp.zeros((TOK, 2 * HEAD), BF)

    def head_out_grad(h, carry):
        hs = pl.ds(pl.multiple_of(h * TOK, TOK), TOK)
        s.part[OUT].g[hs, :] = dot_tn(s.mixed[:, hs], da).astype(BF)
        dq = dot(s.ds[hs, :], kv[:, 0:HEAD]) * HEAD**-0.5
        s.dq[:, hs] = rotate(dq, cos, -sin).astype(BF)
        return carry

    lax.fori_loop(0, HEADS, head_out_grad, 0)

    def swap_halves(src, size, name):
        for b in range(4):
            remote(
                src.at[rows(b * 2 * size + (1 - me.k) * size, size)],
                s.part[name].r0.at[pl.ds(b * size, size)],
                (name, DD),
                sibling,
            )

    swap_halves(s.part[OUT].g, 128, OUT)
    for n in (0, 1):
        s.part[n].g[...] = dot_tn(s.xn[n], s.dq[:, n * 512 : n * 512 + 512]).astype(BF)
        swap_halves(s.part[n].g, 80, n)
    s.dkv[:, 0:HEAD] = dot_tn(s.ds[:, 0:TOK], s.qs[...])
    s.dkv[:, HEAD:] = dot_tn(s.probs[:, 0:TOK], s.dmix[...])

    def merge_halves(name, size, last):
        arrived(s.part[name].r0, (name, DD))
        for b in range(4):
            s.part[name].gs[b * size : b * size + size, :] = (
                s.part[name].g[rows(b * 2 * size + me.k * size, size), :].astype(F32)
                + s.part[name].r0[b * size : b * size + size, :].astype(F32)
            ).astype(BF)
        gather_line(last, s.part[name].gs, size, name)

    merge_halves(OUT, 128, XA)
    merge_halves(0, 80, XA)
    merge_halves(1, 80, YA)

    for back in (2, 1):

        @pl.when(me.ctx + back < 8)
        def _():
            arrived(s.kvrecv.at[pl.ds((back - 1) * TOK, TOK)], (DKV, back))

    dkv = (
        s.dkv[...]
        + s.kvrecv[0:TOK, :].astype(F32)
        + s.kvrecv[TOK : 2 * TOK, :].astype(F32)
    )
    s.dq[:, 1024:1280] = rotate(dkv[:, 0:HEAD], cos, -sin).astype(BF)
    s.dq[:, 1280:1536] = dkv[:, HEAD:].astype(BF)
    s.part[2].g[...] = dot_tn(s.xn[2], s.dq[:, 1024:1536]).astype(BF)
    swap_halves(s.part[2].g, 80, 2)

    def line_sum(name, own, size):
        arrived(s.part[name].r1, (name, E))
        total = own.astype(F32)
        for j in range(3):
            total = total + s.part[name].r1[j * size : j * size + size, :].astype(F32)
        return total.astype(BF)

    def collect_both(name, last):
        total = line_sum(name, s.part[name].g[rows(along(me, last) * 160, 160), :], 160)
        gp = s.part[name].gp
        gp[:, 0:256] = (
            dot_tn(s.pick5[0], total[:, 0:256])
            + dot_tn(s.pick5[1], total[:, 384:640])
            + dot_tn(s.pick5[2], total[:, 768:1024])
        ).astype(BF)
        gp[:, 256:384] = (
            dot_tn(s.pick5[0], total[:, 256:384]) + dot_tn(s.pick5[1], total[:, 640:768])
        ).astype(BF)
        home = s.part[name].r2.at[rows((me.k * 16 + in_plane(last, me.x, me.y, me.z)) * 16, 16)]

        def slot_of(chip, core):
            place = in_plane(last, *chip)
            return place * 2 + core if last == XA else core * 16 + place

        def send(j, carry):
            chip = plane_chip(me, last, j)
            for core in range(2):
                remote(
                    gp.at[rows(slot_of(chip, core) * 16, 16)],
                    home,
                    (name, FR),
                    device(*chip, core),
                )
            return carry

        lax.fori_loop(1, 16, send, 0)
        here = (me.x, me.y, me.z)
        own_copy(gp.at[rows(slot_of(here, me.k) * 16, 16)], home, (name, FR))
        remote(gp.at[rows(slot_of(here, 1 - me.k) * 16, 16)], home, (name, FR), sibling)

    def collect_low(last, src, dst, name, slot_chip):
        home = dst.at[rows(in_plane(last, me.x, me.y, me.z) * 16, 16)]

        def send(i, carry):
            q = lax.rem(i + me.fsdp, 16)
            x, y, z, core = slot_chip(q)
            is_me = (x == me.x) & (y == me.y) & (z == me.z) & (core == me.k)

            @pl.when(is_me)
            def _():
                own_copy(src.at[rows(q * 16, 16)], home, name)

            @pl.when(jnp.logical_not(is_me))
            def _():
                remote(src.at[rows(q * 16, 16)], home, name, device(x, y, z, core))

            return carry

        lax.fori_loop(0, 16, send, 0)

    def collect_same(last, src, dst, name):
        home = dst.at[rows(in_plane(last, me.x, me.y, me.z) * 16, 16)]
        own_copy(src.at[rows(in_plane(last, me.x, me.y, me.z) * 16, 16)], home, name)

        def send(j, carry):
            chip = plane_chip(me, last, j)
            remote(src.at[rows(in_plane(last, *chip) * 16, 16)], home, name, device(*chip, me.k))
            return carry

        lax.fori_loop(1, 16, send, 0)

    def low_chip_x(q):
        return me.x, lax.rem(lax.div(q, 2), 4), 2 * lax.div(q, 8) + me.k, lax.rem(q, 2)

    def low_chip_y(q):
        return lax.div(q, 4), me.y, 2 * lax.rem(lax.div(q, 2), 2) + me.k, lax.rem(q, 2)

    arrived(s.part[DOWN].r1, (DOWN, E))
    for piece in range(8):
        total = s.part[DOWN].g[rows(piece * 128 + me.y * 32, 32), :].astype(F32)
        for j in range(3):
            total = total + s.part[DOWN].r1[j * 256 + piece * 32 : j * 256 + piece * 32 + 32, :].astype(F32)
        s.part[DOWN].gp[piece * 32 : piece * 32 + 32, :] = total.astype(BF)
    collect_low(YA, s.part[DOWN].gp, s.part[DOWN].r2, (DOWN, FR), low_chip_y)
    collect_both(GATE, XA)
    collect_both(UP, ZA)

    total = line_sum(OUT, s.part[OUT].gs[rows(me.x * 128, 128), :], 128)
    s.part[OUT].gp[:, 0:256] = (
        dot_tn(s.pick8[0], total[:, 0:256]) + dot_tn(s.pick8[1], total[:, 384:640])
    ).astype(BF)
    s.part[OUT].gp[:, 256:384] = dot_tn(s.pick8[0], total[:, 256:384]).astype(BF)
    collect_low(XA, s.part[OUT].gp, s.part[OUT].r2, (OUT, FR), low_chip_x)

    merge_halves(2, 80, ZA)

    def collect_qkv(n):
        last = LAST[n]
        name = n
        total = line_sum(name, s.part[name].gs[rows(along(me, last) * 80, 80), :], 80)
        s.part[name].gp[...] = (
            dot_tn(s.pick5[0, 0:80, 0:256], total[:, 0:256])
            + dot_tn(s.pick5[1, 0:80, 0:256], total[:, 256:512])
        ).astype(BF)
        if n == 0:
            collect_low(XA, s.part[0].gp, s.part[0].r2, (0, FR), low_chip_x)
        else:
            collect_same(last, s.part[name].gp, s.part[name].r2, (name, FR))

    collect_qkv(0)
    collect_qkv(1)

    e0 = dot_nt(s.dq[:, 0:512], s.part[0].w[...])
    for n in (1, 2):
        part = dot_nt(s.dq[:, n * 512 : n * 512 + 512], s.part[n].w[...])
        e0 = e0 + dot_nt(part.astype(BF), s.orders[n - 1])
    x = s.xin[...].astype(F32)
    r0 = lax.rsqrt(jnp.mean(x * x, axis=1, keepdims=True) + eps_norm)
    ig[...] = s.dx1[...] + r0 * e0 - x * (r0 * r0 * r0 * jnp.mean(x * e0, axis=1, keepdims=True))
    arrived(s.orecv, OO)
    lo[...] = s.x1[...] + s.outp[0:TOK, :] + s.orecv[...].astype(F32)

    collect_qkv(2)

    def plane_sum(name, out, first):
        total = s.part[name].r2[first * 16 : first * 16 + 16, :].astype(F32)
        for p in range(1, 16):
            total = total + s.part[name].r2[(first + p) * 16 : (first + p) * 16 + 16, :].astype(F32)
        out[first : first + 16, :] = total

    arrived(s.part[DOWN].r2, (DOWN, FR))
    plane_sum(DOWN, sd, 0)
    for name, out in ((GATE, sg), (UP, su)):
        arrived(s.part[name].r2, (name, FR))
        plane_sum(name, out, 0)
        plane_sum(name, out, 16)
    arrived(s.part[OUT].r2, (OUT, FR))
    plane_sum(OUT, so, 0)
    for n, out in ((0, sq0), (1, sq1), (2, sq2)):
        arrived(s.part[n].r2, (n, FR))
        plane_sum(n, out, 0)

    def left_low(ref, name, size):
        @pl.when(me.zl == me.k)
        def _():
            left(ref.at[pl.ds(0, 15 * size)], name)

        @pl.when(me.zl != me.k)
        def _():
            left(ref.at[pl.ds(0, 16 * size)], name)

    left(s.part[2].st.at[pl.ds(0, 240)], (2, A))
    left(s.part[1].st.at[pl.ds(0, 240)], (1, A))
    left_low(s.part[0].st, (0, A), 16)
    left_low(s.part[OUT].st, (OUT, A), 16)
    left_low(s.part[DOWN].w, (DOWN, A), 16)
    for name in (GATE, UP):
        left(s.part[name].st.at[pl.ds(0, 31 * 16)], (name, A))
        left(s.part[name].w.at[pl.ds(0, 480)], (name, B))
        left(s.part[name].r1, (name, E))
        left(s.part[name].r2.at[pl.ds(0, 31 * 16)], (name, FR))
    for n in range(3):
        left(s.part[n].w.at[pl.ds(0, 240)], (n, B))
        left(s.part[n].w.at[pl.ds(0, 320)], (n, C))
        left(s.part[n].r0, (n, DD))
        left(s.part[n].r1, (n, E))
    left_low(s.part[0].r2, (0, FR), 16)
    left(s.part[1].r2.at[pl.ds(0, 240)], (1, FR))
    left(s.part[2].r2.at[pl.ds(0, 240)], (2, FR))
    left(s.part[OUT].w.at[pl.ds(0, 384)], (OUT, B))
    left(s.part[OUT].w.at[pl.ds(0, 512)], (OUT, C))
    left(s.part[OUT].r0, (OUT, DD))
    left(s.part[OUT].r1, (OUT, E))
    left_low(s.part[OUT].r2, (OUT, FR), 16)
    left(s.part[DOWN].w.at[pl.ds(0, 768)], (DOWN, B))
    left(s.part[DOWN].r1, (DOWN, E))
    left_low(s.part[DOWN].r2, (DOWN, FR), 16)
    left(s.cin, DY)
    left(s.esend, EE)
    left(s.osend, OO)
    left(s.osend, X2)
    for back in (1, 2):

        @pl.when(me.ctx + back < 8)
        def _():
            left(kv.at[pl.ds(0, TOK)], (KV, back))

        @pl.when(me.ctx >= back)
        def _():
            left(s.kvsend.at[pl.ds(0, TOK)], (DKV, back))

    assert len(sems) <= SEMS


def whole_step(tokens, cotangent, starts, wq, wo, wgu, wd, gains):
    orders, pick5, pick8, rope = constants()
    scratch = scratch_list()
    vmem = pl.BlockSpec(memory_space=pltpu.VMEM)
    anywhere = pl.BlockSpec(memory_space=pl.ANY)
    smem = pl.BlockSpec(memory_space=pltpu.SMEM)
    shapes = [(TOK, D), (TOK, D)] + [(16, 256)] * 3 + [(16, 384), (32, 384), (32, 384), (16, 640)]
    return pl.pallas_call(
        functools.partial(step_kernel, scratch),
        name="whole_step",
        out_shape=[jax.ShapeDtypeStruct(shape, F32) for shape in shapes],
        in_specs=[anywhere, anywhere, smem] + [vmem] * 5 + [anywhere] * 4,
        out_specs=[vmem] * len(shapes),
        scratch_shapes=leaves(scratch)
        + [
            pltpu.SemaphoreType.DMA((8,)),
            pltpu.SemaphoreType.DMA((SEMS,)),
            pltpu.SemaphoreType.DMA((SEMS,)),
        ],
        compiler_params=pltpu.CompilerParams(
            collective_id=0, has_side_effects=True, vmem_limit_bytes=62 * 2**20
        ),
        cost_estimate=pl.CostEstimate(
            flops=12_000_000_000, bytes_accessed=8_000_000, transcendentals=2_000_000
        ),
    )(tokens, cotangent, starts, wq, wo, wgu, wd, gains, orders, pick5, pick8, rope)


def adamw(master, first, second, gradient, rate, decay):
    first_next = beta_one * first + (1.0 - beta_one) * gradient
    second_next = beta_two * second + (1.0 - beta_two) * gradient * gradient
    first_fixed = first_next * (1.0 / (1.0 - beta_one**STEP))
    second_fixed = second_next * (1.0 / (1.0 - beta_two**STEP))
    update = first_fixed / (jnp.sqrt(second_fixed) + eps_adam) + decay * master
    return master - rate * update, first_next, second_next


def update_kernel(*refs):
    inner = refs[41:65]
    sem = refs[65]
    copies = [
        pltpu.make_async_copy(src, dst, sem.at[n])
        for n, (src, dst) in enumerate(zip(refs[:24], inner))
    ]
    for one in copies:
        one.start()
    (sq0, sq1, sq2, so, sg, su, sd) = inner[2:9]
    (wq, qf, qs, wo, of, os_, wgu, gf, gs, wd, df, ds_, gains, nf, ns) = inner[9:]
    (oq, oqf, oqs, oo, oof, oos, og, ogf, ogs, od, odf, ods, on, onf, ons) = refs[26:41]
    for one in copies:
        one.wait()
    through = [
        pltpu.make_async_copy(inner[n], refs[24 + n].at[0], sem.at[24 + n]) for n in range(2)
    ]
    for one in through:
        one.start()

    rate = 1.5 * D**-0.5
    gain0 = column(gains[0:1, :])
    gain1 = column(gains[1:2, :])
    total0 = jnp.zeros((5, 1), F32)
    for n, share in enumerate((sq0, sq1, sq2)):
        for g in range(2):
            at = slice(n * 512 + g * 256, n * 512 + g * 256 + 256)
            raw = share[5 * g : 5 * g + 5, :]
            w = wq[:, at]
            total0 = total0 + jnp.sum(w.astype(BF).astype(F32) * raw, axis=1, keepdims=True)
            oq[:, at], oqf[:, at], oqs[:, at] = adamw(
                w, qf[:, at], qs[:, at], raw * gain0, rate, weight_decay
            )
    total1 = jnp.zeros((5, 1), F32)
    for n, share in enumerate((sg, su)):
        for c in range(2):
            for t in range(8):
                g, i = t // 3, t % 3
                base = n * FF + (t // 2) * 512 + c * 256 + (t % 2) * 128
                at = slice(base, base + 128)
                raw = share[c * 16 + 5 * g : c * 16 + 5 * g + 5, i * 128 : i * 128 + 128]
                w = wgu[:, at]
                total1 = total1 + jnp.sum(w.astype(BF).astype(F32) * raw, axis=1, keepdims=True)
                og[:, at], ogf[:, at], ogs[:, at] = adamw(
                    w, gf[:, at], gs[:, at], raw * gain1, rate, weight_decay
                )
    rate = 1.5 * OUT_FAN**-0.5
    for r, at in ((0, slice(0, 384)), (8, slice(384, 640))):
        raw = so[r : r + 8, 0 : at.stop - at.start]
        oo[:, at], oof[:, at], oos[:, at] = adamw(
            wo[:, at], of[:, at], os_[:, at], raw, rate, weight_decay
        )
    od[...], odf[...], ods[...] = adamw(
        wd[...], df[...], ds_[...], sd[...], 1.5 * FF**-0.5, weight_decay
    )
    i = lax.broadcasted_iota(jnp.int32, (5, 5), 0)
    j = lax.broadcasted_iota(jnp.int32, (5, 5), 1)
    for row, total in ((0, total0), (1, total1)):
        flat = jnp.sum(jnp.where(i == j, jnp.broadcast_to(total, (5, 5)), 0.0), axis=0, keepdims=True)
        at = slice(row, row + 1)
        on[at, :], onf[at, :], ons[at, :] = adamw(gains[at, :], nf[at, :], ns[at, :], flat, 0.5, 0.0)
    for one in through:
        one.wait()


def update(*arrays):
    vmem = pl.BlockSpec(memory_space=pltpu.VMEM)
    anywhere = pl.BlockSpec(memory_space=pl.ANY)
    outs = [jax.ShapeDtypeStruct((1, TOK, D), F32)] * 2 + [
        jax.ShapeDtypeStruct(a.shape, F32) for a in arrays[9:]
    ]
    return pl.pallas_call(
        update_kernel,
        name="update",
        out_shape=outs,
        in_specs=[anywhere] * len(arrays),
        out_specs=[anywhere] * 2 + [vmem] * (len(outs) - 2),
        scratch_shapes=[pltpu.VMEM(a.shape, F32) for a in arrays]
        + [pltpu.SemaphoreType.DMA((len(arrays) + 2,))],
        compiler_params=pltpu.CompilerParams(vmem_limit_bytes=60 * 2**20),
    )(*arrays)


def body(
    tokens,
    cotangent,
    starts,
    qkv_weight,
    qkv_first,
    qkv_second,
    out_weight,
    out_first,
    out_second,
    gate_up_weight,
    gate_up_first,
    gate_up_second,
    down_weight,
    down_first,
    down_second,
    norm_gains,
    gains_first,
    gains_second,
):
    results = whole_step(
        tokens, cotangent, starts, qkv_weight, out_weight, gate_up_weight, down_weight, norm_gains
    )
    return tuple(
        update(
            *results,
            qkv_weight,
            qkv_first,
            qkv_second,
            out_weight,
            out_first,
            out_second,
            gate_up_weight,
            gate_up_first,
            gate_up_second,
            down_weight,
            down_first,
            down_second,
            norm_gains,
            gains_first,
            gains_second,
        )
    )


def solution(mesh):
    act = P("fsdp", "ctx", None)
    row = P(("ctx", "fsdp"), None)
    gain = P(None, ("ctx", "fsdp"))
    return jax.shard_map(
        body,
        mesh=mesh,
        in_specs=(act, act, P("fsdp")) + (row,) * 12 + (gain,) * 3,
        out_specs=(act, act) + (row,) * 12 + (gain,) * 3,
        check_vma=False,
    )
```

time: 1730 us -> 130 us (0.08)
  waiting for transfers between devices: 1340 us -> 0 us
  blocking collectives: 244 us -> 0 us
  Pallas kernels: 0 us -> 127 us
  matrix products: 54.3 us -> 0 us
  other arithmetic: 26.8 us -> 0 us
  local copies, waits for them, and re-layouts: 21.9 us -> 0 us
  starting transfers between devices: 17.9 us -> 0 us
    reduce_scatter x1 -> x0, waiting for transfers between devices: 634 us -> none  [body(): lax.psum_scatter(grad_down, ('ctx', 'fsdp'), scatter_dimension=0, tiled=T...]
    all_gather x4 -> x0, waiting for transfers between devices: 562 us -> none  [the longest x1 200 us: body(): lax.all_gather(gate_up_weight.astype(jnp.bfloat16), ('ctx', 'fsdp'), axis...]
    all_gather x1 -> x0, blocking collectives: 179 us -> none  [body(): lax.all_gather(norm_gains.astype(jnp.bfloat16), ('ctx', 'fsdp'), axis=1,...]
    unnamed x7 -> x0, waiting for transfers between devices: 140 us -> none
    pallas_call x0 -> x2, Pallas kernels: none -> 127 us  [the longest x1 123 us: whole_step(): pl.pallas_call(functools.partial(step_kernel, scratch), name='whole_step'...]
    unnamed x1 -> x0, blocking collectives: 64.8 us -> none
    dot_general x18 -> x0, matrix products: 54.3 us -> none  [the longest x1 6.56 us: body(): jnp.dot(second_normed, gate_up_matrix, preferred_element_type=jnp.float32)]
    ppermute x8 -> x0, starting transfers between devices: 17.7 us -> none  [shifted(): return lax.ppermute(block, axis, route)]
  transfers between devices with their start and end apart: 14 -> 0, of which waited for: 8 -> 0; matrix products, arithmetic and copies ran while one was open for 4% -> 0% of each run, Pallas kernels for 0% -> 0%
where the time goes in v1:
time: 130 us; the launch traced here: 129 us
  Pallas kernels  127 us (98%)
  between operations  1.47 us (1%)
    pallas_call x1, Pallas kernels, whole_step(): pl.pallas_call(functools.partial(step_kernel, scratch), name='whole_step'...  123 us
    pallas_call x1, Pallas kernels, update(): pl.pallas_call(update_kernel, name='update', out_shape=outs, in_specs=[an...  3.8 us

profile of v1, /device:TPU:1, one launch (start us, length us, event | category | flops | bytes accessed | tf_op | source)
XLA Modules:
  0.0 128.7 jit_solution(12979749742744810268)
XLA Ops:
  1.3 123.5 %whole_step.1 = (f32[256,640]{1,0:T(8,128)}, f32[256,640]{1,0:T(8,128)}, f32[16,256]{1,0:T(8,128)}, f32[16,256]{1,0:T(8,128)}, f32[16,256]{1,0:T(8,128)}, /*inde...) custom-call(bf16[1,256,640]{2,1,0:T(8,128)(2,1)} %refs_0_.1, ...), custom_call_target="tpu_custom_call" | custom-call | flops 12000000000 | bytes 8000000 | tf_op jit(solution)/shard_map/whole_step/pallas_call | solution.py:911
  124.8 3.8 %update.1 = (f32[1,256,640]{2,1,0:T(8,128)}, f32[1,256,640]{2,1,0:T(8,128)}, f32[5,1536]{1,0:T(8,128)}, f32[5,1536]{1,0:T(8,128)}, f32[5,1536]{1,0:T(8,128)}, /*...) custom-call(f32[256,640]{1,0:T(8,128)} %get-tuple-element.26.refs_0_, ...), custom_call_target="tpu_custom_call" | custom-call | tf_op jit(solution)/shard_map/update/pallas_call | solution.py:1012

commit v2 on v1

v2 whole, which is shorter than its diff:
```python
import functools

import jax
import jax.numpy as jnp
import numpy as np
from jax import lax
from jax.experimental import pallas as pl
from jax.experimental.pallas import tpu as pltpu
from jax.sharding import PartitionSpec as P

D = 640
HEADS = 4
HEAD = 256
FF = 2048
WINDOW = 512
STEP = 10
QW = 1024
OUT_FAN = 8
TOK = 256
LENGTH = 2048

eps_norm = 1e-06
beta_one = 0.9
beta_two = 0.95
eps_adam = 1e-08
weight_decay = 0.1
masked_score = -1e30

MESH = pl.DeviceIdType.MESH
BF = jnp.bfloat16
F32 = jnp.float32


class Place:
    def __init__(self):
        self.ctx = lax.axis_index("ctx")
        self.fsdp = lax.axis_index("fsdp")
        self.x = lax.div(self.ctx, 2)
        self.zl = lax.rem(self.ctx, 2)
        self.zh = lax.div(self.fsdp, 8)
        self.y = lax.div(lax.rem(self.fsdp, 8), 2)
        self.k = lax.rem(self.fsdp, 2)
        self.z = 2 * self.zh + self.zl


def device(x, y, z, k):
    return (2 * x + lax.rem(z, 2), 8 * lax.div(z, 2) + 2 * y + k)


def around(a, b):
    return lax.rem(a + b, 4)


def plane_chip(me, last, j):
    a, b = lax.rem(j, 4), lax.div(j, 4)
    if last == XA:
        return me.x, around(me.y, a), around(me.z, b)
    if last == YA:
        return around(me.x, a), me.y, around(me.z, b)
    return around(me.x, a), around(me.y, b), me.z


def line_chip(me, last, j):
    if last == XA:
        return around(me.x, j), me.y, me.z
    if last == YA:
        return me.x, around(me.y, j), me.z
    return me.x, me.y, around(me.z, j)


def along(me, last):
    return (me.x, me.y, me.z)[last]


def in_plane(last, x, y, z):
    if last == XA:
        return lax.rem(z, 2) * 8 + lax.div(z, 2) * 4 + y
    if last == YA:
        return 4 * x + z
    return 4 * x + y


def rows(start, size):
    return pl.ds(pl.multiple_of(start, 16), size)


def feature_order(last):
    order = np.zeros(D, np.int64)
    for x in range(4):
        for y in range(4):
            for z in range(4):
                for k in range(2):
                    dev = x * 32 + (z % 2) * 16 + (z // 2) * 8 + y * 2 + k
                    b, p = (y, 4 * x + z) if last == YA else (z, 4 * y + x)
                    for r in range(5):
                        order[b * 160 + k * 80 + p * 5 + r] = 5 * dev + r
    return order


def constants():
    orders = np.zeros((2, D, D), np.float32)
    for n, last in enumerate((YA, ZA)):
        orders[n, feature_order(last), np.arange(D)] = 1.0
    pick5 = np.zeros((3, 160, 512), np.float32)
    for g in range(3):
        for s in range(32):
            for r in range(5):
                pick5[g, s * 5 + r, s * 16 + g * 5 + r] = 1.0
    pick8 = np.zeros((2, 128, 256), np.float32)
    for g in range(2):
        for s in range(16):
            for r in range(8):
                pick8[g, s * 8 + r, s * 16 + g * 8 + r] = 1.0
    half = HEAD // 2
    frequency = np.float32(10000.0) ** (
        -(np.float32(2.0) * np.arange(half, dtype=np.float32)) / np.float32(HEAD)
    )
    angles = np.arange(LENGTH, dtype=np.float32)[:, None] * frequency.astype(np.float32)[None, :]
    rope = np.stack([np.cos(angles.astype(np.float64)), np.sin(angles.astype(np.float64))])
    return (
        jnp.asarray(orders, BF),
        jnp.asarray(pick5, BF),
        jnp.asarray(pick8, BF),
        jnp.asarray(rope.astype(np.float32)),
    )


def dot(a, b):
    return lax.dot_general(a, b, (((1,), (0,)), ((), ())), preferred_element_type=F32)


def dot_nt(a, b):
    return lax.dot_general(a, b, (((1,), (1,)), ((), ())), preferred_element_type=F32)


def dot_tn(a, b):
    return lax.dot_general(a, b, (((0,), (0,)), ((), ())), preferred_element_type=F32)


def rotate(u, cos, sin):
    a, b = u[:, :128], u[:, 128:]
    return jnp.concatenate([a * cos - b * sin, b * cos + a * sin], axis=1)


def column(row):
    n = row.shape[1]
    i = lax.broadcasted_iota(jnp.int32, (n, n), 0)
    j = lax.broadcasted_iota(jnp.int32, (n, n), 1)
    wide = jnp.broadcast_to(row.astype(BF).astype(F32), (n, n))
    return jnp.sum(jnp.where(i == j, wide, 0.0), axis=1, keepdims=True)


class Bag(dict):
    __getattr__ = dict.__getitem__


def scratch_list():
    def v(*shape, kind=BF):
        return pltpu.VMEM(shape, kind)

    qkv = [
        Bag(
            pk=v(16, 256),
            st=v(256, 256),
            w=v(640, 512),
            g=v(640, 512),
            r0=v(320, 512),
            gs=v(320, 512),
            r1=v(240, 512),
            gp=v(256, 256),
            ra=v(192, 256),
            ga=v(64, 256),
            rb=v(64, 256),
        )
        for n in range(3)
    ]
    out = Bag(
        pk=v(16, 384),
        st=v(256, 384),
        w=v(1024, 640),
        g=v(1024, 640),
        r0=v(512, 640),
        gs=v(512, 640),
        r1=v(384, 640),
        gp=v(256, 384),
        ra=v(192, 384),
        ga=v(64, 384),
        rb=v(64, 384),
    )
    gate_up = [
        Bag(
            pk=v(32, 384),
            st=v(512, 384),
            w=v(640, 1024),
            g=v(640, 1024),
            rf=v(160, 1024),
            sf=v(160, 1024),
            r1=v(320, 1024),
            gp=v(512, 384),
            ra=v(384, 384),
            ga=v(128, 384),
            rb=v(128, 384),
        )
        for n in range(2)
    ]
    down = Bag(
        pk=v(16, 640),
        w=v(1024, 640),
        g=v(1024, 640),
        rf=v(256, 640),
        sf=v(256, 640),
        r1=v(512, 640),
        gp=v(256, 640),
        ra=v(192, 640),
        ga=v(64, 640),
        rb=v(64, 640),
    )
    return Bag(
        part=qkv + [out] + gate_up + [down],
        tokens=v(3 * TOK, D),
        cin=v(TOK, D),
        orders=v(2, D, D),
        pick5=v(3, 160, 512),
        pick8=v(2, 128, 256),
        rope=v(3, 2, TOK, 128, kind=F32),
        pad=v(16, 384, kind=F32),
        xn=v(2, TOK, D),
        xnz=v(3 * TOK, D),
        qs=v(HEADS * TOK, HEAD),
        kv=v(3 * TOK, 2 * HEAD),
        bias=v(TOK, 3 * TOK, kind=F32),
        probs=v(HEADS * TOK, 3 * TOK),
        ds=v(HEADS * TOK, 3 * TOK),
        mixed=v(TOK, QW),
        dmix=v(HEADS * TOK, HEAD),
        x1=v(TOK, D, kind=F32),
        x2=v(2 * TOK, D),
        x2z=v(2 * TOK, D),
        dy2=v(2 * TOK, D),
        outp=v(2 * TOK, D, kind=F32),
        ex=v(2 * TOK, D, kind=F32),
        ez=v(2 * TOK, D, kind=F32),
        osend=v(TOK, D),
        orecv=v(TOK, D),
        esend=v(TOK, D),
        erecv=v(TOK, D),
        dx1=v(TOK, D, kind=F32),
        dq=v(TOK, QW),
        dkv=v(3 * TOK, 2 * HEAD),
        dkvr=v(3 * TOK, 2 * HEAD),
        dkvs=v(TOK, 2 * HEAD),
    )


def leaves(tree):
    if isinstance(tree, dict):
        return [leaf for branch in tree.values() for leaf in leaves(branch)]
    if isinstance(tree, list):
        return [leaf for branch in tree for leaf in leaves(branch)]
    return [tree]


def refill(tree, values):
    if isinstance(tree, dict):
        return Bag({key: refill(branch, values) for key, branch in tree.items()})
    if isinstance(tree, list):
        return [refill(branch, values) for branch in tree]
    return next(values)


OUT, GATE, UP, DOWN = 3, 4, 5, 6
XA, YA, ZA = range(3)
LAST = (XA, YA, ZA, ZA, XA, ZA, YA)
A1, A2, B1, B2, C, D1, E1, E2, F1, F2 = range(10)
DY, X2, EE, OO, TK, DKV = range(7, 13)
SEMS = 128


def wait_for(ref, sem):
    pltpu.make_async_copy(ref, ref, sem).wait()


def step_kernel(shape, *refs):
    (tok, cot, starts, wq, wo, wgu, wd, gains, orders_h, pick5_h, pick8_h, rope_h) = refs[:12]
    (lo, ig, sq0, sq1, sq2, so, sg, su, sd) = refs[12:21]
    s = refill(shape, iter(refs[21:-3]))
    local, sent, came = refs[-3:]
    me = Place()
    sems = {}
    taken = [0]

    def sem_of(name, size=1):
        if name not in sems:
            sems[name] = taken[0]
            taken[0] += size
        return sems[name]

    def remote(src, dst, name, target, tile=None):
        n = sem_of(name, 1 if tile is None else 4)
        pltpu.make_async_remote_copy(
            src_ref=src,
            dst_ref=dst,
            send_sem=sent.at[n],
            recv_sem=came.at[n if tile is None else n + tile],
            device_id=target,
            device_id_type=MESH,
        ).start()

    def own_copy(src, dst, name):
        pltpu.make_async_copy(src, dst, came.at[sem_of(name)]).start()

    def arrived(ref, name, tile=0):
        wait_for(ref, came.at[sem_of(name) + tile])

    def left(ref, name):
        wait_for(ref, sent.at[sem_of(name)])

    sibling = device(me.x, me.y, me.z, 1 - me.k)

    fetch = [
        (tok.at[0], s.tokens.at[pl.ds(0, TOK)]),
        (orders_h, s.orders),
        (pick5_h, s.pick5),
        (pick8_h, s.pick8),
        (cot.at[0], s.cin),
        (cot.at[0], s.dy2.at[pl.ds(0, TOK)]),
    ]
    for back in range(3):
        block = jnp.maximum(me.ctx - back, 0) * TOK
        fetch.append((rope_h.at[:, pl.ds(pl.multiple_of(block, TOK), TOK), :], s.rope.at[back]))
    fetches = [pltpu.make_async_copy(a, b, local.at[n]) for n, (a, b) in enumerate(fetch)]
    for one in fetches:
        one.start()

    barrier = pltpu.get_barrier_semaphore()
    for j in range(1, 4):
        for axis in range(3):
            for core in range(2):
                pl.semaphore_signal(
                    barrier,
                    inc=1,
                    device_id=device(*line_chip(me, axis, j), core),
                    device_id_type=MESH,
                )
    pl.semaphore_signal(barrier, inc=1, device_id=sibling, device_id_type=MESH)

    pad = s.pad
    pad[...] = jnp.zeros((16, 384), F32)
    wqb = wq[...].astype(BF).astype(F32) * column(gains[0:1, :])
    for n in range(3):
        for g in range(2):
            pad[5 * g : 5 * g + 5, 0:256] = wqb[:, n * 512 + g * 256 : n * 512 + g * 256 + 256]
        s.part[n].pk[...] = pad[:, 0:256].astype(BF)
    gain = column(gains[1:2, :])
    for n, name in enumerate((GATE, UP)):
        for c in range(2):
            for t in range(8):
                g, i = t // 3, t % 3
                base = n * FF + (t // 2) * 512 + c * 256 + (t % 2) * 128
                pad[5 * g : 5 * g + 5, i * 128 : i * 128 + 128] = (
                    wgu[:, base : base + 128].astype(BF).astype(F32) * gain
                )
            pad[10:15, 256:384] = jnp.zeros((5, 128), F32)
            s.part[name].pk[c * 16 : c * 16 + 16, :] = pad[...].astype(BF)
    pad[0:8, :] = wo[:, 0:384]
    pad[8:16, 0:256] = wo[:, 384:640]
    pad[8:16, 256:384] = jnp.zeros((8, 128), F32)
    s.part[OUT].pk[...] = pad[...].astype(BF)
    s.part[DOWN].pk[...] = wd[...].astype(BF)
    fetches[0].wait()
    pl.semaphore_wait(barrier, 19)

    def to_line(axis, src, dst, name, core):
        for j in (1, 3, 2):
            remote(src, dst, name, device(*line_chip(me, axis, j), core))

    def to_line_core(axis, src, dst, name, core):
        to_line(axis, src, dst, name, core)

        @pl.when(core == me.k)
        def _():
            own_copy(src, dst, name)

        @pl.when(core != me.k)
        def _():
            remote(src, dst, name, sibling)

    def to_line_both(axis, src, dst, name):
        for j in (1, 3, 2):
            for core in range(2):
                remote(
                    src.at[pl.ds(core * 16, 16)], dst, name, device(*line_chip(me, axis, j), core)
                )
        own_copy(src.at[rows(me.k * 16, 16)], dst, name)
        remote(src.at[rows((1 - me.k) * 16, 16)], dst, name, sibling)

    xh, xl = lax.div(me.x, 2), lax.rem(me.x, 2)
    zi = me.zl * 2 + me.zh
    part = s.part
    place = part[2].st.at[rows((4 * me.y + me.x) * 16, 16)]
    own_copy(part[2].pk, place, (2, A1))
    to_line(XA, part[2].pk, place, (2, A1), me.k)
    place = part[1].st.at[rows((4 * me.x + me.z) * 16, 16)]
    own_copy(part[1].pk, place, (1, A1))
    to_line(ZA, part[1].pk, place, (1, A1), me.k)
    low_slot = (me.zh * 4 + me.y) * 2 + me.k
    to_line_core(ZA, part[0].pk, part[0].st.at[rows(low_slot * 16, 16)], (0, A1), me.zl)

    def block(ref, back):
        return ref.at[pl.ds(back * TOK, TOK)]

    @pl.when(me.ctx < 6)
    def _():
        remote(block(s.tokens, 0), block(s.tokens, 2), (TK, 2), (me.ctx + 2, me.fsdp))

    @pl.when(me.zl == 0)
    def _():
        remote(block(s.tokens, 0), block(s.tokens, 1), (TK, 1), (me.ctx + 1, me.fsdp))

    def first_norm(rows_in):
        field = rows_in.astype(F32)
        r = lax.rsqrt(jnp.mean(field * field, axis=1, keepdims=True) + eps_norm)
        return (field * r).astype(BF)

    xn = first_norm(s.tokens[0:TOK, :])
    s.xn[0] = xn
    for n in range(1, len(fetches)):
        fetches[n].wait()
    s.xn[1] = dot(xn, s.orders[0]).astype(BF)
    s.xnz[0:TOK, :] = dot(xn, s.orders[1]).astype(BF)

    def pieces_on(axis, ref, starts_, size, name):
        for j in (1, 3, 2):
            for start in starts_:
                at = ref.at[rows(start, size)]
                remote(at, at, name, device(*line_chip(me, axis, j), me.k))

    arrived(part[2].st.at[pl.ds(0, 64)], (2, A1))
    pieces_on(YA, part[2].st, [me.y * 64], 64, (2, A2))
    arrived(part[1].st.at[pl.ds(0, 64)], (1, A1))
    pieces_on(XA, part[1].st, [me.x * 64], 64, (1, A2))
    arrived(part[0].st.at[pl.ds(0, 64)], (0, A1))
    pieces_on(YA, part[0].st, [(zh * 4 + me.y) * 32 for zh in range(2)], 32, (0, A2))
    remote(s.cin, block(s.dy2, 1), DY, sibling)
    out_slot = (xl * 4 + me.y) * 2 + me.k
    to_line_core(XA, part[OUT].pk, part[OUT].st.at[rows(out_slot * 16, 16)], (OUT, A1), xh)
    gate_slot = (zi * 4 + me.y) * 2 + me.k
    to_line_both(ZA, part[GATE].pk, part[GATE].st.at[rows(gate_slot * 16, 16)], (GATE, A1))
    up_slot = me.k * 16 + me.y * 4 + me.x
    to_line_both(XA, part[UP].pk, part[UP].st.at[rows(up_slot * 16, 16)], (UP, A1))
    down_row = me.x * 256 + me.zh * 128 + me.y * 32 + me.k * 16
    to_line_core(ZA, part[DOWN].pk, part[DOWN].w.at[rows(down_row, 16)], (DOWN, A1), me.zl)

    for n in (2, 1, 0):
        arrived(part[n].st.at[pl.ds(0, 192)], (n, A2))
        start = along(me, LAST[n]) * 160 + me.k * 80
        st = part[n].st[...]
        for g in range(2):
            part[n].w[rows(start, 80), g * 256 : g * 256 + 256] = dot(
                s.pick5[g, 0:80, 0:256], st
            ).astype(BF)
        pieces_on(LAST[n], part[n].w, [start], 80, (n, B1))

    arrived(part[OUT].st.at[pl.ds(0, 64)], (OUT, A1))
    pieces_on(YA, part[OUT].st, [(n * 4 + me.y) * 32 for n in range(2)], 32, (OUT, A2))
    arrived(part[GATE].st.at[pl.ds(0, 128)], (GATE, A1))
    pieces_on(YA, part[GATE].st, [(n * 4 + me.y) * 32 for n in range(4)], 32, (GATE, A2))
    arrived(part[UP].st.at[pl.ds(0, 128)], (UP, A1))
    pieces_on(YA, part[UP].st, [n * 256 + me.y * 64 for n in range(2)], 64, (UP, A2))
    arrived(part[DOWN].w.at[pl.ds(0, 64)], (DOWN, A1))
    pieces_on(
        XA, part[DOWN].w, [me.x * 256 + n * 128 + me.y * 32 for n in range(2)], 32, (DOWN, A2)
    )

    def columns(t):
        return pl.ds(pl.multiple_of(t * 256, 256), 256)

    def tile_of(name, b, t):
        if name == DOWN:
            return [rows(t * 256 + zh * 128 + b * 32, 32) for zh in range(2)]
        return [(rows(b * 160, 160), columns(t))]

    def tile_step(t):
        return 1 + 2 * lax.rem(t, 2)

    def start_tiles(name):
        b = along(me, LAST[name])
        ref = part[name].w
        for t in range(4):
            ahead = 1 + 2 * (t % 2)
            for at in tile_of(name, b, t):
                for stage, j in ((B1, ahead), (B2, 4 - ahead)):
                    target = device(*line_chip(me, LAST[name], j), me.k)
                    remote(ref.at[at], ref.at[at], (name, stage), target, t)

    def pass_tile(name, t):
        j = tile_step(t)
        b = around(along(me, LAST[name]), 4 - j)
        ref = part[name].w
        target = device(*line_chip(me, LAST[name], j), me.k)
        size = tile_bytes(name, 1)
        arrived(size, (name, B1), t)
        for at in tile_of(name, b, t):
            remote(ref.at[at], ref.at[at], (name, B2), target, t)

    def tile_bytes(name, count):
        if name == DOWN:
            return part[name].w.at[pl.ds(0, 64 * count)]
        return part[name].w.at[pl.ds(0, 160 * count), pl.ds(0, 256)]

    def out_rows(z):
        return [rows((2 * me.k + n) * 256 + lax.rem(z, 2) * 128 + lax.div(z, 2) * 64, 64) for n in range(2)]

    def start_out():
        for n in range(2):
            at = part[OUT].w.at[out_rows(me.z)[n]]
            for stage, j in ((B1, 1 + 2 * n), (B2, 3 - 2 * n)):
                remote(at, at, (OUT, stage), device(*line_chip(me, ZA, j), me.k), n)

    def pass_out():
        for n in range(2):
            at = part[OUT].w.at[out_rows(around(me.z, 3 - 2 * n))[n]]
            arrived(part[OUT].w.at[pl.ds(0, 64)], (OUT, B1), n)
            remote(at, at, (OUT, B2), device(*line_chip(me, ZA, 1 + 2 * n), me.k), n)

    def unpack5(name):
        start = along(me, LAST[name]) * 160
        st = part[name].st[...]
        for g in range(3):
            width = 384 if g < 2 else 256
            part[name].w[rows(start, 160), g * 384 : g * 384 + width] = dot(
                s.pick5[g], st[:, 0:width]
            ).astype(BF)

    for back in (1, 2):

        @pl.when(me.ctx < back)
        def _():
            s.tokens[back * TOK : back * TOK + TOK, :] = jnp.zeros((TOK, D), BF)

    @pl.when(me.ctx >= 2)
    def _():
        arrived(block(s.tokens, 2), (TK, 2))

    @pl.when((me.zl == 1) & (me.ctx >= 2))
    def _():
        remote(block(s.tokens, 2), block(s.tokens, 1), (TK, 1), (me.ctx - 1, me.fsdp))

    for n in (2, 1, 0):
        arrived(part[n].w.at[pl.ds(0, 240)], (n, B1))
        for b in range(4):
            at = part[n].w.at[rows(b * 160 + me.k * 80, 80)]
            remote(at, at, (n, C), sibling)

    arrived(part[OUT].st.at[pl.ds(0, 192)], (OUT, A2))
    st = part[OUT].st[...]
    left_cols = dot(s.pick8[0], st).astype(BF)
    right_cols = dot(s.pick8[1], st[:, 0:256]).astype(BF)
    for n in range(2):
        part[OUT].w[out_rows(me.z)[n], 0:384] = left_cols[n * 64 : n * 64 + 64, :]
        part[OUT].w[out_rows(me.z)[n], 384:640] = right_cols[n * 64 : n * 64 + 64, :]
    start_out()
    arrived(part[GATE].st.at[pl.ds(0, 384)], (GATE, A2))
    unpack5(GATE)
    start_tiles(GATE)
    arrived(part[UP].st.at[pl.ds(0, 384)], (UP, A2))
    unpack5(UP)
    start_tiles(UP)
    arrived(part[DOWN].w.at[pl.ds(0, 192)], (DOWN, A2))
    start_tiles(DOWN)

    s.xnz[2 * TOK :, :] = dot(first_norm(s.tokens[2 * TOK :, :]), s.orders[1]).astype(BF)

    boundary = starts[0]
    qi = lax.broadcasted_iota(jnp.int32, (TOK, TOK), 0)
    kj = lax.broadcasted_iota(jnp.int32, (TOK, TOK), 1)
    query_place = me.ctx * TOK + qi
    query_doc = (query_place >= boundary).astype(jnp.int32)
    for back in range(3):
        key_place = (me.ctx - back) * TOK + kj
        gap = query_place - key_place
        key_doc = (key_place >= boundary).astype(jnp.int32)
        allowed = (gap >= 0) & (gap < WINDOW) & (key_place >= 0) & (query_doc == key_doc)
        s.bias[:, back * TOK : back * TOK + TOK] = jnp.where(allowed, 0.0, masked_score)

    kv = s.kv
    cos = s.rope[0, 0]
    sin = s.rope[0, 1]
    for n in (1, 0):
        arrived(part[n].w.at[pl.ds(0, 320)], (n, C))
        field = dot(s.xn[n], part[n].w[...])
        for i in range(2):
            h = 2 * n + i
            s.qs[h * TOK : h * TOK + TOK, :] = (
                rotate(field[:, i * HEAD : i * HEAD + HEAD], cos, sin) * HEAD**-0.5
            ).astype(BF)

    def keys_values(back):
        at = slice(back * TOK, back * TOK + TOK)
        field = dot(s.xnz[at, :], part[2].w[...])
        kv[at, 0:HEAD] = rotate(field[:, 0:HEAD], s.rope[back, 0], s.rope[back, 1]).astype(BF)
        kv[at, HEAD:] = field[:, HEAD:].astype(BF)

    arrived(part[2].w.at[pl.ds(0, 320)], (2, C))
    keys_values(0)
    keys_values(2)

    @pl.when(me.ctx >= 1)
    def _():
        arrived(block(s.tokens, 1), (TK, 1))

    s.xnz[TOK : 2 * TOK, :] = dot(first_norm(s.tokens[TOK : 2 * TOK, :]), s.orders[1]).astype(BF)
    keys_values(1)

    def head_forward(h, carry):
        hs = pl.ds(pl.multiple_of(h * TOK, TOK), TOK)
        scores = dot_nt(s.qs[hs, :], kv[:, 0:HEAD]) + s.bias[...]
        top = jnp.max(scores, axis=1, keepdims=True)
        e = jnp.exp(scores - top)
        p = (e * (1.0 / jnp.sum(e, axis=1, keepdims=True))).astype(BF)
        s.probs[hs, :] = p
        s.mixed[:, hs] = dot(p, kv[:, HEAD:]).astype(BF)
        for name in (GATE, UP, DOWN):
            pass_tile(name, h)
        return carry

    pass_out()
    lax.fori_loop(0, HEADS, head_forward, 0)
    for n in range(2):
        arrived(part[OUT].w.at[pl.ds(0, 128)], (OUT, B2), n)
    half = part[OUT].w.at[rows(me.k * 512, 512)]
    remote(half, half, (OUT, C), sibling)

    x = s.tokens[0:TOK, :].astype(F32)
    arrived(part[OUT].w.at[pl.ds(0, 512)], (OUT, C))
    x1 = x + dot(s.mixed[...], part[OUT].w[...])
    s.x1[...] = x1
    r1 = lax.rsqrt(jnp.mean(x1 * x1, axis=1, keepdims=True) + eps_norm)
    s.x2[0:TOK, :] = (x1 * r1).astype(BF)
    remote(block(s.x2, 0), block(s.x2, 1), X2, sibling)
    arrived(block(s.dy2, 1), DY)
    s.outp[...] = jnp.zeros((2 * TOK, D), F32)
    s.ex[...] = jnp.zeros((2 * TOK, D), F32)
    s.ez[...] = jnp.zeros((2 * TOK, D), F32)
    s.x2z[0:TOK, :] = dot(s.x2[0:TOK, :], s.orders[1]).astype(BF)
    arrived(block(s.x2, 1), X2)
    s.x2z[TOK:, :] = dot(s.x2[TOK:, :], s.orders[1]).astype(BF)

    root = 0.7978845608028654

    def sum_at(name, t):
        if name == DOWN:
            return [rows(t * 64 + zh * 32, 32) for zh in range(2)]
        return [(pl.ds(0, 160), columns(t))]

    def start_sums(name, t):
        j = tile_step(t)
        b = along(me, LAST[name])
        size = 160 if name != DOWN else 256
        for stage, step, source, dst in (
            (E1, j, around(b, 2), part[name].rf),
            (E2, 4 - j, around(b, 4 - j), part[name].r1.at[pl.ds(0, size)]),
        ):
            target = device(*line_chip(me, LAST[name], step), me.k)
            for at, to in zip(tile_of(name, source, t), sum_at(name, t)):
                remote(part[name].g.at[at], dst.at[to], (name, stage), target, t)

    def pass_sums(name, t):
        j = tile_step(t)
        source = around(along(me, LAST[name]), j)
        size = 160 if name != DOWN else 256
        target = device(*line_chip(me, LAST[name], j), me.k)
        arrived(tile_bytes(name, 1), (name, E1), t)
        for at, to in zip(tile_of(name, source, t), sum_at(name, t)):
            part[name].sf[to] = (
                part[name].g[at].astype(F32) + part[name].rf[to].astype(F32)
            ).astype(BF)
            remote(
                part[name].sf.at[to],
                part[name].r1.at[pl.ds(size, size)].at[to],
                (name, E2),
                target,
                t,
            )

    def hidden_step(t, carry):
        for name in (GATE, UP, DOWN):
            arrived(tile_bytes(name, 2), (name, B2), t)
        ts = columns(t)
        w_g, w_u, w_d = part[GATE].w, part[UP].w, part[DOWN].w
        gate = dot(s.x2[...], w_g[:, ts])
        up = dot(s.x2z[...], w_u[:, ts])
        d_hidden = dot_nt(s.dy2[...], w_d[ts, :])
        square = gate * gate
        th = jnp.tanh(root * gate * (1.0 + 0.044715 * square))
        half = 0.5 * (1.0 + th)
        act = gate * half
        slope = half + 0.5 * gate * (1.0 - th * th) * (root * (1.0 + 0.134145 * square))
        hidden = (act * up).astype(BF)
        d_gate = (d_hidden * up * slope).astype(BF)
        d_up = (d_hidden * act).astype(BF)
        part[DOWN].g[ts, :] = dot_tn(hidden, s.dy2[...]).astype(BF)
        part[GATE].g[:, ts] = dot_tn(s.x2[...], d_gate).astype(BF)
        part[UP].g[:, ts] = dot_tn(s.x2z[...], d_up).astype(BF)
        for name in (GATE, UP, DOWN):
            start_sums(name, t)
        s.outp[...] += dot(hidden, w_d[ts, :])
        s.ex[...] += dot_nt(d_gate, w_g[:, ts])
        s.ez[...] += dot_nt(d_up, w_u[:, ts])
        return carry

    lax.fori_loop(0, 4, hidden_step, 0)

    other = s.ex[TOK:, :] + dot_nt(s.ez[TOK:, :].astype(BF), s.orders[1])
    s.esend[...] = other.astype(BF)
    remote(s.esend, s.erecv, EE, sibling)
    s.osend[...] = s.outp[TOK:, :].astype(BF)
    remote(s.osend, s.orecv, OO, sibling)
    e1 = s.ex[0:TOK, :] + dot_nt(s.ez[0:TOK, :].astype(BF), s.orders[1])
    arrived(s.erecv, EE)
    e1 = e1 + s.erecv[...].astype(F32)
    x1 = s.x1[...]
    r1 = lax.rsqrt(jnp.mean(x1 * x1, axis=1, keepdims=True) + eps_norm)
    dx1 = (
        s.cin[...].astype(F32)
        + r1 * e1
        - x1 * (r1 * r1 * r1 * jnp.mean(x1 * e1, axis=1, keepdims=True))
    )
    s.dx1[...] = dx1
    da = dx1.astype(BF)

    def head_backward(h, carry):
        hs = pl.ds(pl.multiple_of(h * TOK, TOK), TOK)
        dmix = dot_nt(da, part[OUT].w[hs, :]).astype(BF)
        s.dmix[hs, :] = dmix
        d_probs = dot_nt(dmix, kv[:, HEAD:])
        p = s.probs[hs, :].astype(F32)
        center = jnp.sum(p * d_probs, axis=1, keepdims=True)
        s.ds[hs, :] = (p * (d_probs - center)).astype(BF)
        for name in (GATE, UP, DOWN):
            pass_sums(name, h)
        return carry

    lax.fori_loop(0, HEADS, head_backward, 0)

    for back in (2, 1, 0):
        at = slice(back * TOK, back * TOK + TOK)
        dk = dot_tn(s.ds[:, at], s.qs[...])
        s.dkv[at, 0:HEAD] = rotate(dk, s.rope[back, 0], -s.rope[back, 1]).astype(BF)
        s.dkv[at, HEAD:] = dot_tn(s.probs[:, at], s.dmix[...]).astype(BF)

    def swap_halves(n):
        for b in range(4):
            remote(
                part[n].g.at[rows(b * 160 + (1 - me.k) * 80, 80)],
                part[n].r0.at[pl.ds(b * 80, 80)],
                (n, D1),
                sibling,
            )

    part[2].g[...] = dot_tn(s.xnz[...], s.dkv[...]).astype(BF)
    swap_halves(2)

    @pl.when((me.zl == 0) & (me.ctx >= 2))
    def _():
        remote(block(s.dkv, 1), block(s.dkvr, 0), (DKV, 0), (me.ctx + 1, me.fsdp))
        remote(block(s.dkv, 2), block(s.dkvr, 2), (DKV, 2), (me.ctx - 2, me.fsdp))

    @pl.when(me.zl == 1)
    def _():
        remote(block(s.dkv, 1), block(s.dkvr, 1), (DKV, 1), (me.ctx - 1, me.fsdp))

    def head_query(h, carry):
        hs = pl.ds(pl.multiple_of(h * TOK, TOK), TOK)
        dq = dot(s.ds[hs, :], kv[:, 0:HEAD]) * HEAD**-0.5
        s.dq[:, hs] = rotate(dq, cos, -sin).astype(BF)
        part[OUT].g[hs, :] = dot_tn(s.mixed[:, hs], da).astype(BF)
        return carry

    lax.fori_loop(0, HEADS, head_query, 0)
    for n in (1, 0):
        part[n].g[...] = dot_tn(s.xn[n], s.dq[:, n * 512 : n * 512 + 512]).astype(BF)
        swap_halves(n)
    remote(part[OUT].g.at[rows((1 - me.k) * 512, 512)], part[OUT].r0, (OUT, D1), sibling)

    def scatter(n, axis, starts_of, size):
        for j in (1, 3, 2):
            chip = line_chip(me, axis, j)
            starts_ = starts_of(*chip)
            for i, start in enumerate(starts_):
                remote(
                    part[n].gp.at[rows(start, size)],
                    part[n].ra.at[pl.ds(((j - 1) * len(starts_) + i) * size, size)],
                    (n, F1),
                    device(*chip, me.k),
                )

    def gathered(n, starts_of, size):
        starts_ = starts_of(me.x, me.y, me.z)
        total = size * len(starts_)
        arrived(part[n].ra, (n, F1))
        for i, start in enumerate(starts_):
            rows_here = part[n].gp[rows(start, size), :].astype(F32)
            for j in range(3):
                at = j * total + i * size
                rows_here = rows_here + part[n].ra[at : at + size, :].astype(F32)
            part[n].ga[i * size : i * size + size, :] = rows_here.astype(BF)

    def q0_rows(x, y, z):
        return [(n * 4 + y) * 32 for n in range(2)]

    def q1_rows(x, y, z):
        return [x * 64]

    def q2_rows(x, y, z):
        return [y * 64]

    def gate_rows(x, y, z):
        return [(n * 4 + y) * 32 for n in range(4)]

    def up_rows(x, y, z):
        return [n * 256 + y * 64 for n in range(2)]

    plane_of = {
        0: (YA, q0_rows, 32),
        1: (XA, q1_rows, 64),
        2: (YA, q2_rows, 64),
        OUT: (YA, q0_rows, 32),
        GATE: (YA, gate_rows, 32),
        UP: (YA, up_rows, 64),
        DOWN: (XA, q1_rows, 64),
    }

    for name in (GATE, UP, DOWN):
        for t in range(4):
            arrived(tile_bytes(name, 2), (name, E2), t)
        r1 = part[name].r1
        if name == DOWN:
            for n in range(8):
                at = slice(n * 32, n * 32 + 32)
                part[DOWN].gp[at, :] = (
                    part[DOWN].g[rows(n * 128 + me.y * 32, 32), :].astype(F32)
                    + r1[at, :].astype(F32)
                    + r1[256 + n * 32 : 256 + n * 32 + 32, :].astype(F32)
                ).astype(BF)
        else:
            total = (
                part[name].g[rows(along(me, LAST[name]) * 160, 160), :].astype(F32)
                + r1[0:160, :].astype(F32)
                + r1[160:320, :].astype(F32)
            ).astype(BF)
            part[name].gp[:, 0:256] = (
                dot_tn(s.pick5[0], total[:, 0:256])
                + dot_tn(s.pick5[1], total[:, 384:640])
                + dot_tn(s.pick5[2], total[:, 768:1024])
            ).astype(BF)
            part[name].gp[:, 256:384] = (
                dot_tn(s.pick5[0], total[:, 256:384]) + dot_tn(s.pick5[1], total[:, 640:768])
            ).astype(BF)
        scatter(name, *plane_of[name])

    def to_blocks(n, starts_of, size):
        for j in (1, 3, 2):
            b = around(along(me, LAST[n]), j)
            for i, start in enumerate(starts_of(b)):
                remote(
                    part[n].gs.at[rows(start, size)],
                    part[n].r1.at[pl.ds(((j - 1) * len(starts_of(b)) + i) * size, size)],
                    (n, E1),
                    device(*line_chip(me, LAST[n], j), me.k),
                )

    def qkv_rows(b):
        return [b * 80]

    def out_half_rows(b):
        return [n * 256 + lax.rem(b, 2) * 128 + lax.div(b, 2) * 64 for n in range(2)]

    for n in (2, 1, 0):
        arrived(part[n].r0, (n, D1))
        for b in range(4):
            at = slice(b * 80, b * 80 + 80)
            part[n].gs[at, :] = (
                part[n].g[rows(b * 160 + me.k * 80, 80), :].astype(F32)
                + part[n].r0[at, :].astype(F32)
            ).astype(BF)
        to_blocks(n, qkv_rows, 80)
    arrived(part[OUT].r0, (OUT, D1))
    part[OUT].gs[...] = (
        part[OUT].g[rows(me.k * 512, 512), :].astype(F32) + part[OUT].r0[...].astype(F32)
    ).astype(BF)
    to_blocks(OUT, out_half_rows, 64)

    def owners_same(n, axis):
        home = part[n].rb.at[rows(along(me, axis) * 16, 16)]
        own_copy(part[n].ga.at[rows(along(me, axis) * 16, 16)], home, (n, F2))
        for j in (1, 3, 2):
            chip = line_chip(me, axis, j)
            remote(
                part[n].ga.at[rows(chip[axis] * 16, 16)],
                home,
                (n, F2),
                device(*chip, me.k),
            )

    def owners_low(n, axis):
        home = part[n].rb.at[rows(along(me, axis) * 16, 16)]
        for i in range(2):
            for core in range(2):
                if axis == ZA:
                    chip = (me.x, me.y, 2 * i + me.k)
                    here = chip[2] == me.z
                else:
                    chip = (2 * me.k + i, me.y, me.z)
                    here = chip[0] == me.x
                src = part[n].ga.at[pl.ds((i * 2 + core) * 16, 16)]
                mine = here & (me.k == core)

                @pl.when(mine)
                def _():
                    own_copy(src, home, (n, F2))

                @pl.when(jnp.logical_not(mine))
                def _():
                    remote(src, home, (n, F2), device(*chip, core))

    def owners_both(n, axis, slot_of):
        home = part[n].rb.at[rows((me.k * 4 + along(me, axis)) * 16, 16)]
        for j in (0, 1, 3, 2):
            chip = line_chip(me, axis, j)
            for flip in range(2):
                core = lax.rem(me.k + flip, 2)
                src = part[n].ga.at[rows(slot_of(chip[axis], core) * 16, 16)]
                if j == 0 and flip == 0:
                    own_copy(src, home, (n, F2))
                else:
                    remote(src, home, (n, F2), device(*chip, core))

    def spread_owners(n):
        gathered(n, *plane_of[n][1:])
        if n == 1:
            owners_same(1, ZA)
        elif n == 2:
            owners_same(2, XA)
        elif n == GATE:
            owners_both(n, ZA, lambda z, core: (lax.rem(z, 2) * 2 + lax.div(z, 2)) * 2 + core)
        elif n == UP:
            owners_both(n, XA, lambda place, core: core * 4 + place)
        else:
            owners_low(n, XA if n == OUT else ZA)

    for name in (GATE, UP, DOWN):
        spread_owners(name)

    for n in (2, 1, 0):
        arrived(part[n].r1, (n, E1))
        total = part[n].gs[rows(along(me, LAST[n]) * 80, 80), :].astype(F32)
        for j in range(3):
            total = total + part[n].r1[j * 80 : j * 80 + 80, :].astype(F32)
        total = total.astype(BF)
        part[n].gp[...] = (
            dot_tn(s.pick5[0, 0:80, 0:256], total[:, 0:256])
            + dot_tn(s.pick5[1, 0:80, 0:256], total[:, 256:512])
        ).astype(BF)
        scatter(n, *plane_of[n])

    arrived(part[OUT].r1, (OUT, E1))
    halves = []
    for i, start in enumerate(out_half_rows(me.z)):
        total = part[OUT].gs[rows(start, 64), :].astype(F32)
        for j in range(3):
            at = (j * 2 + i) * 64
            total = total + part[OUT].r1[at : at + 64, :].astype(F32)
        halves.append(total.astype(BF))
    total = jnp.concatenate(halves, axis=0)
    part[OUT].gp[:, 0:256] = (
        dot_tn(s.pick8[0], total[:, 0:256]) + dot_tn(s.pick8[1], total[:, 384:640])
    ).astype(BF)
    part[OUT].gp[:, 256:384] = dot_tn(s.pick8[0], total[:, 256:384]).astype(BF)
    scatter(OUT, *plane_of[OUT])

    @pl.when((me.zl == 1) & (me.ctx >= 2))
    def _():
        arrived(block(s.dkvr, 0), (DKV, 0))
        s.dkvs[...] = (s.dkv[2 * TOK :, :].astype(F32) + s.dkvr[0:TOK, :].astype(F32)).astype(BF)
        remote(s.dkvs, block(s.dkvr, 2), (DKV, 2), (me.ctx - 2, me.fsdp))

    e0 = dot_nt(s.dq[:, 0:512], part[0].w[...])
    field = dot_nt(s.dq[:, 512:1024], part[1].w[...])
    e0 = e0 + dot_nt(field.astype(BF), s.orders[0])
    s.ex[0:TOK, :] = e0
    arrived(s.orecv, OO)
    lo[...] = s.x1[...] + s.outp[0:TOK, :] + s.orecv[...].astype(F32)

    for n in (2, 1, 0, OUT):
        spread_owners(n)

    @pl.when(me.ctx < 6)
    def _():
        arrived(block(s.dkvr, 2), (DKV, 2))

    @pl.when(me.ctx >= 6)
    def _():
        s.dkvr[2 * TOK :, :] = jnp.zeros((TOK, 2 * HEAD), BF)

    @pl.when(me.zl == 0)
    def _():
        arrived(block(s.dkvr, 1), (DKV, 1))

    @pl.when(me.zl == 1)
    def _():
        s.dkvr[TOK : 2 * TOK, :] = jnp.zeros((TOK, 2 * HEAD), BF)

    dkv = (
        s.dkv[0:TOK, :].astype(F32)
        + s.dkvr[TOK : 2 * TOK, :].astype(F32)
        + s.dkvr[2 * TOK :, :].astype(F32)
    ).astype(BF)
    field = dot_nt(dkv, part[2].w[...])
    e0 = s.ex[0:TOK, :] + dot_nt(field.astype(BF), s.orders[1])
    x = s.tokens[0:TOK, :].astype(F32)
    r0 = lax.rsqrt(jnp.mean(x * x, axis=1, keepdims=True) + eps_norm)
    ig[...] = s.dx1[...] + r0 * e0 - x * (r0 * r0 * r0 * jnp.mean(x * e0, axis=1, keepdims=True))

    def line_total(n, out, first):
        base = first * 4
        total = part[n].rb[base : base + 16, :].astype(F32)
        for p in range(1, 4):
            total = total + part[n].rb[base + p * 16 : base + p * 16 + 16, :].astype(F32)
        out[first : first + 16, :] = total

    for n, out in ((GATE, sg), (UP, su), (DOWN, sd), (2, sq2), (1, sq1), (0, sq0), (OUT, so)):
        arrived(part[n].rb, (n, F2))
        line_total(n, out, 0)
        if n in (GATE, UP):
            line_total(n, out, 16)

    def left_or(condition, ref, name, low, high):
        @pl.when(condition)
        def _():
            left(ref.at[pl.ds(0, low)], name)

        @pl.when(jnp.logical_not(condition))
        def _():
            left(ref.at[pl.ds(0, high)], name)

    for n in range(7):
        p = part[n]
        home = {0: me.zl, OUT: xh, DOWN: me.zl}
        if n in home:
            left_or(home[n] == me.k, p.gp, (n, A1), 48, 64)
            left_or(home[n] == me.k, p.gp, (n, F2), 48, 64)
        elif n in (GATE, UP):
            left(p.st.at[pl.ds(0, 7 * 16)], (n, A1))
            left(p.rb.at[pl.ds(0, 7 * 16)], (n, F2))
        else:
            left(p.st.at[pl.ds(0, 48)], (n, A1))
            left(p.rb.at[pl.ds(0, 48)], (n, F2))
        left(p.ra, (n, F1))
    for n in range(3):
        left(part[n].st.at[pl.ds(0, 192)], (n, A2))
        left(part[n].w.at[pl.ds(0, 240)], (n, B1))
        left(part[n].w.at[pl.ds(0, 320)], (n, C))
        left(part[n].r0, (n, D1))
        left(part[n].r1, (n, E1))
    left(part[OUT].st.at[pl.ds(0, 192)], (OUT, A2))
    left(part[OUT].w.at[pl.ds(0, 128)], (OUT, B1))
    left(part[OUT].w.at[pl.ds(0, 256)], (OUT, B2))
    left(part[OUT].w.at[pl.ds(0, 512)], (OUT, C))
    left(part[OUT].r0, (OUT, D1))
    left(part[OUT].r1, (OUT, E1))
    for name in (GATE, UP, DOWN):
        if name == DOWN:
            left(part[name].w.at[pl.ds(0, 192)], (name, A2))
        else:
            left(part[name].st.at[pl.ds(0, 384)], (name, A2))
        block_rows = 256 if name == DOWN else 160
        left(part[name].w.at[pl.ds(0, block_rows)], (name, B1))
        left(part[name].w.at[pl.ds(0, 2 * block_rows)], (name, B2))
        left(part[name].w.at[pl.ds(0, block_rows)], (name, E1))
        left(part[name].w.at[pl.ds(0, 2 * block_rows)], (name, E2))
    left(s.cin, DY)
    left(s.esend, EE)
    left(s.osend, OO)
    left(s.osend, X2)

    @pl.when(me.ctx < 6)
    def _():
        left(block(s.tokens, 0), (TK, 2))

    @pl.when((me.zl == 0) | (me.ctx >= 2))
    def _():
        left(block(s.tokens, 0), (TK, 1))

    @pl.when((me.zl == 0) & (me.ctx >= 2))
    def _():
        left(s.dkvs, (DKV, 0))

    @pl.when(me.ctx >= 2)
    def _():
        left(s.dkvs, (DKV, 2))

    @pl.when(me.zl == 1)
    def _():
        left(s.dkvs, (DKV, 1))

    assert taken[0] <= SEMS


def whole_step(tokens, cotangent, starts, wq, wo, wgu, wd, gains):
    orders, pick5, pick8, rope = constants()
    scratch = scratch_list()
    vmem = pl.BlockSpec(memory_space=pltpu.VMEM)
    anywhere = pl.BlockSpec(memory_space=pl.ANY)
    smem = pl.BlockSpec(memory_space=pltpu.SMEM)
    shapes = [(TOK, D), (TOK, D)] + [(16, 256)] * 3 + [(16, 384), (32, 384), (32, 384), (16, 640)]
    return pl.pallas_call(
        functools.partial(step_kernel, scratch),
        name="whole_step",
        out_shape=[jax.ShapeDtypeStruct(shape, F32) for shape in shapes],
        in_specs=[anywhere, anywhere, smem] + [vmem] * 5 + [anywhere] * 4,
        out_specs=[vmem] * len(shapes),
        scratch_shapes=leaves(scratch)
        + [
            pltpu.SemaphoreType.DMA((12,)),
            pltpu.SemaphoreType.DMA((SEMS,)),
            pltpu.SemaphoreType.DMA((SEMS,)),
        ],
        compiler_params=pltpu.CompilerParams(
            collective_id=0, has_side_effects=True, vmem_limit_bytes=62 * 2**20
        ),
        cost_estimate=pl.CostEstimate(
            flops=12_000_000_000, bytes_accessed=8_000_000, transcendentals=2_000_000
        ),
    )(tokens, cotangent, starts, wq, wo, wgu, wd, gains, orders, pick5, pick8, rope)


def adamw(master, first, second, gradient, rate, decay):
    first_next = beta_one * first + (1.0 - beta_one) * gradient
    second_next = beta_two * second + (1.0 - beta_two) * gradient * gradient
    first_fixed = first_next * (1.0 / (1.0 - beta_one**STEP))
    second_fixed = second_next * (1.0 / (1.0 - beta_two**STEP))
    update = first_fixed / (jnp.sqrt(second_fixed) + eps_adam) + decay * master
    return master - rate * update, first_next, second_next


def update_kernel(*refs):
    inner = refs[41:65]
    sem = refs[65]
    copies = [
        pltpu.make_async_copy(src, dst, sem.at[n])
        for n, (src, dst) in enumerate(zip(refs[:24], inner))
    ]
    for one in copies:
        one.start()
    (sq0, sq1, sq2, so, sg, su, sd) = inner[2:9]
    (wq, qf, qs, wo, of, os_, wgu, gf, gs, wd, df, ds_, gains, nf, ns) = inner[9:]
    (oq, oqf, oqs, oo, oof, oos, og, ogf, ogs, od, odf, ods, on, onf, ons) = refs[26:41]
    for one in copies:
        one.wait()
    through = [
        pltpu.make_async_copy(inner[n], refs[24 + n].at[0], sem.at[24 + n]) for n in range(2)
    ]
    for one in through:
        one.start()

    rate = 1.5 * D**-0.5
    gain0 = column(gains[0:1, :])
    gain1 = column(gains[1:2, :])
    total0 = jnp.zeros((5, 1), F32)
    for n, share in enumerate((sq0, sq1, sq2)):
        for g in range(2):
            at = slice(n * 512 + g * 256, n * 512 + g * 256 + 256)
            raw = share[5 * g : 5 * g + 5, :]
            w = wq[:, at]
            total0 = total0 + jnp.sum(w.astype(BF).astype(F32) * raw, axis=1, keepdims=True)
            oq[:, at], oqf[:, at], oqs[:, at] = adamw(
                w, qf[:, at], qs[:, at], raw * gain0, rate, weight_decay
            )
    total1 = jnp.zeros((5, 1), F32)
    for n, share in enumerate((sg, su)):
        for c in range(2):
            for t in range(8):
                g, i = t // 3, t % 3
                base = n * FF + (t // 2) * 512 + c * 256 + (t % 2) * 128
                at = slice(base, base + 128)
                raw = share[c * 16 + 5 * g : c * 16 + 5 * g + 5, i * 128 : i * 128 + 128]
                w = wgu[:, at]
                total1 = total1 + jnp.sum(w.astype(BF).astype(F32) * raw, axis=1, keepdims=True)
                og[:, at], ogf[:, at], ogs[:, at] = adamw(
                    w, gf[:, at], gs[:, at], raw * gain1, rate, weight_decay
                )
    rate = 1.5 * OUT_FAN**-0.5
    for r, at in ((0, slice(0, 384)), (8, slice(384, 640))):
        raw = so[r : r + 8, 0 : at.stop - at.start]
        oo[:, at], oof[:, at], oos[:, at] = adamw(
            wo[:, at], of[:, at], os_[:, at], raw, rate, weight_decay
        )
    od[...], odf[...], ods[...] = adamw(
        wd[...], df[...], ds_[...], sd[...], 1.5 * FF**-0.5, weight_decay
    )
    i = lax.broadcasted_iota(jnp.int32, (5, 5), 0)
    j = lax.broadcasted_iota(jnp.int32, (5, 5), 1)
    for row, total in ((0, total0), (1, total1)):
        flat = jnp.sum(jnp.where(i == j, jnp.broadcast_to(total, (5, 5)), 0.0), axis=0, keepdims=True)
        at = slice(row, row + 1)
        on[at, :], onf[at, :], ons[at, :] = adamw(gains[at, :], nf[at, :], ns[at, :], flat, 0.5, 0.0)
    for one in through:
        one.wait()


def update(*arrays):
    vmem = pl.BlockSpec(memory_space=pltpu.VMEM)
    anywhere = pl.BlockSpec(memory_space=pl.ANY)
    outs = [jax.ShapeDtypeStruct((1, TOK, D), F32)] * 2 + [
        jax.ShapeDtypeStruct(a.shape, F32) for a in arrays[9:]
    ]
    return pl.pallas_call(
        update_kernel,
        name="update",
        out_shape=outs,
        in_specs=[anywhere] * len(arrays),
        out_specs=[anywhere] * 2 + [vmem] * (len(outs) - 2),
        scratch_shapes=[pltpu.VMEM(a.shape, F32) for a in arrays]
        + [pltpu.SemaphoreType.DMA((len(arrays) + 2,))],
        compiler_params=pltpu.CompilerParams(vmem_limit_bytes=60 * 2**20),
    )(*arrays)


def body(
    tokens,
    cotangent,
    starts,
    qkv_weight,
    qkv_first,
    qkv_second,
    out_weight,
    out_first,
    out_second,
    gate_up_weight,
    gate_up_first,
    gate_up_second,
    down_weight,
    down_first,
    down_second,
    norm_gains,
    gains_first,
    gains_second,
):
    results = whole_step(
        tokens, cotangent, starts, qkv_weight, out_weight, gate_up_weight, down_weight, norm_gains
    )
    return tuple(
        update(
            *results,
            qkv_weight,
            qkv_first,
            qkv_second,
            out_weight,
            out_first,
            out_second,
            gate_up_weight,
            gate_up_first,
            gate_up_second,
            down_weight,
            down_first,
            down_second,
            norm_gains,
            gains_first,
            gains_second,
        )
    )


def solution(mesh):
    act = P("fsdp", "ctx", None)
    row = P(("ctx", "fsdp"), None)
    gain = P(None, ("ctx", "fsdp"))
    return jax.shard_map(
        body,
        mesh=mesh,
        in_specs=(act, act, P("fsdp")) + (row,) * 12 + (gain,) * 3,
        out_specs=(act, act) + (row,) * 12 + (gain,) * 3,
        check_vma=False,
    )
```

time: 130 us -> 108 us (0.83)
  Pallas kernels: 127 us -> 106 us
    pallas_call x1, Pallas kernels: 123 us -> 102 us  [whole_step(): pl.pallas_call(functools.partial(step_kernel, scratch), name='whole_step'...]
where the time goes in v2:
time: 108 us; the launch traced here: 107 us
  Pallas kernels  106 us (98%)
  between operations  1.49 us (1%)
    pallas_call x1, Pallas kernels, whole_step(): pl.pallas_call(functools.partial(step_kernel, scratch), name='whole_step'...  102 us
    pallas_call x1, Pallas kernels, update(): pl.pallas_call(update_kernel, name='update', out_shape=outs, in_specs=[an...  3.8 us

profile of v2, /device:TPU:1, one launch (start us, length us, event | category | flops | bytes accessed | tf_op | source)
XLA Modules:
  0.0 107.4 jit_solution(12604262271030066114)
XLA Ops:
  1.3 102.1 %whole_step.1 = (f32[256,640]{1,0:T(8,128)}, f32[256,640]{1,0:T(8,128)}, f32[16,256]{1,0:T(8,128)}, f32[16,256]{1,0:T(8,128)}, f32[16,256]{1,0:T(8,128)}, /*inde...) custom-call(bf16[1,256,640]{2,1,0:T(8,128)(2,1)} %refs_0_.1, ...), custom_call_target="tpu_custom_call" | custom-call | flops 12000000000 | bytes 8000000 | tf_op jit(solution)/shard_map/whole_step/pallas_call | solution.py:1117
  103.4 3.8 %update.1 = (f32[1,256,640]{2,1,0:T(8,128)}, f32[1,256,640]{2,1,0:T(8,128)}, f32[5,1536]{1,0:T(8,128)}, f32[5,1536]{1,0:T(8,128)}, f32[5,1536]{1,0:T(8,128)}, /*...) custom-call(f32[256,640]{1,0:T(8,128)} %get-tuple-element.26.refs_0_, ...), custom_call_target="tpu_custom_call" | custom-call | tf_op jit(solution)/shard_map/update/pallas_call | solution.py:1218

commit v3 on v2

--- a/solution.py
+++ b/solution.py
@@ -237,9 +237,11 @@
         x2=v(2 * TOK, D),
         x2z=v(2 * TOK, D),
         dy2=v(2 * TOK, D),
-        outp=v(2 * TOK, D, kind=F32),
-        ex=v(2 * TOK, D, kind=F32),
-        ez=v(2 * TOK, D, kind=F32),
+        hidden=v(2 * TOK, FF // 2),
+        d_gate=v(2 * TOK, FF // 2),
+        d_up=v(2 * TOK, FF // 2),
+        outp=v(TOK, D, kind=F32),
+        e0=v(TOK, D, kind=F32),
         osend=v(TOK, D),
         orecv=v(TOK, D),
         esend=v(TOK, D),
@@ -445,7 +447,7 @@
     out_slot = (xl * 4 + me.y) * 2 + me.k
     to_line_core(XA, part[OUT].pk, part[OUT].st.at[rows(out_slot * 16, 16)], (OUT, A1), xh)
     gate_slot = (zi * 4 + me.y) * 2 + me.k
-    to_line_both(ZA, part[GATE].pk, part[GATE].st.at[rows(gate_slot * 16, 16)], (GATE, A1))
+    to_line_both(YA, part[GATE].pk, part[GATE].st.at[rows(gate_slot * 16, 16)], (GATE, A1))
     up_slot = me.k * 16 + me.y * 4 + me.x
     to_line_both(XA, part[UP].pk, part[UP].st.at[rows(up_slot * 16, 16)], (UP, A1))
     down_row = me.x * 256 + me.zh * 128 + me.y * 32 + me.k * 16
@@ -464,7 +466,7 @@
     arrived(part[OUT].st.at[pl.ds(0, 64)], (OUT, A1))
     pieces_on(YA, part[OUT].st, [(n * 4 + me.y) * 32 for n in range(2)], 32, (OUT, A2))
     arrived(part[GATE].st.at[pl.ds(0, 128)], (GATE, A1))
-    pieces_on(YA, part[GATE].st, [(n * 4 + me.y) * 32 for n in range(4)], 32, (GATE, A2))
+    pieces_on(ZA, part[GATE].st, [zi * 128], 128, (GATE, A2))
     arrived(part[UP].st.at[pl.ds(0, 128)], (UP, A1))
     pieces_on(YA, part[UP].st, [n * 256 + me.y * 64 for n in range(2)], 64, (UP, A2))
     arrived(part[DOWN].w.at[pl.ds(0, 64)], (DOWN, A1))
@@ -612,24 +614,26 @@
     s.xnz[TOK : 2 * TOK, :] = dot(first_norm(s.tokens[TOK : 2 * TOK, :]), s.orders[1]).astype(BF)
     keys_values(1)
 
-    def head_forward(h, carry):
-        hs = pl.ds(pl.multiple_of(h * TOK, TOK), TOK)
+    def head_forward(h):
+        hs = slice(h * TOK, h * TOK + TOK)
         scores = dot_nt(s.qs[hs, :], kv[:, 0:HEAD]) + s.bias[...]
         top = jnp.max(scores, axis=1, keepdims=True)
         e = jnp.exp(scores - top)
         p = (e * (1.0 / jnp.sum(e, axis=1, keepdims=True))).astype(BF)
         s.probs[hs, :] = p
         s.mixed[:, hs] = dot(p, kv[:, HEAD:]).astype(BF)
-        for name in (GATE, UP, DOWN):
-            pass_tile(name, h)
-        return carry
 
     pass_out()
-    lax.fori_loop(0, HEADS, head_forward, 0)
-    for n in range(2):
-        arrived(part[OUT].w.at[pl.ds(0, 128)], (OUT, B2), n)
-    half = part[OUT].w.at[rows(me.k * 512, 512)]
-    remote(half, half, (OUT, C), sibling)
+    for h in range(HEADS):
+        if h >= 2:
+            for name in (GATE, UP, DOWN):
+                pass_tile(name, h - 2)
+        if h == 2:
+            for n in range(2):
+                arrived(part[OUT].w.at[pl.ds(0, 128)], (OUT, B2), n)
+            half = part[OUT].w.at[rows(me.k * 512, 512)]
+            remote(half, half, (OUT, C), sibling)
+        head_forward(h)
 
     x = s.tokens[0:TOK, :].astype(F32)
     arrived(part[OUT].w.at[pl.ds(0, 512)], (OUT, C))
@@ -638,10 +642,10 @@
     r1 = lax.rsqrt(jnp.mean(x1 * x1, axis=1, keepdims=True) + eps_norm)
     s.x2[0:TOK, :] = (x1 * r1).astype(BF)
     remote(block(s.x2, 0), block(s.x2, 1), X2, sibling)
+    for t in (2, 3):
+        for name in (GATE, UP, DOWN):
+            pass_tile(name, t)
     arrived(block(s.dy2, 1), DY)
-    s.outp[...] = jnp.zeros((2 * TOK, D), F32)
-    s.ex[...] = jnp.zeros((2 * TOK, D), F32)
-    s.ez[...] = jnp.zeros((2 * TOK, D), F32)
     s.x2z[0:TOK, :] = dot(s.x2[0:TOK, :], s.orders[1]).astype(BF)
     arrived(block(s.x2, 1), X2)
     s.x2z[TOK:, :] = dot(s.x2[TOK:, :], s.orders[1]).astype(BF)
@@ -704,19 +708,29 @@
         part[UP].g[:, ts] = dot_tn(s.x2z[...], d_up).astype(BF)
         for name in (GATE, UP, DOWN):
             start_sums(name, t)
-        s.outp[...] += dot(hidden, w_d[ts, :])
-        s.ex[...] += dot_nt(d_gate, w_g[:, ts])
-        s.ez[...] += dot_nt(d_up, w_u[:, ts])
+        s.hidden[:, ts] = hidden
+        s.d_gate[:, ts] = d_gate
+        s.d_up[:, ts] = d_up
         return carry
 
     lax.fori_loop(0, 4, hidden_step, 0)
 
-    other = s.ex[TOK:, :] + dot_nt(s.ez[TOK:, :].astype(BF), s.orders[1])
-    s.esend[...] = other.astype(BF)
+    def from_hidden(at):
+        far = dot_nt(s.d_up[at, :], part[UP].w[...]).astype(BF)
+        return dot_nt(s.d_gate[at, :], part[GATE].w[...]) + dot_nt(far, s.orders[1])
+
+    s.esend[...] = from_hidden(slice(TOK, 2 * TOK)).astype(BF)
     remote(s.esend, s.erecv, EE, sibling)
-    s.osend[...] = s.outp[TOK:, :].astype(BF)
+    for t in (0, 1):
+        for name in (GATE, UP, DOWN):
+            pass_sums(name, t)
+    e1 = from_hidden(slice(0, TOK))
+    for t in (2, 3):
+        for name in (GATE, UP, DOWN):
+            pass_sums(name, t)
+    s.osend[...] = dot(s.hidden[TOK:, :], part[DOWN].w[...]).astype(BF)
     remote(s.osend, s.orecv, OO, sibling)
-    e1 = s.ex[0:TOK, :] + dot_nt(s.ez[0:TOK, :].astype(BF), s.orders[1])
+    s.outp[...] = s.x1[...] + dot(s.hidden[0:TOK, :], part[DOWN].w[...])
     arrived(s.erecv, EE)
     e1 = e1 + s.erecv[...].astype(F32)
     x1 = s.x1[...]
@@ -729,6 +743,14 @@
     s.dx1[...] = dx1
     da = dx1.astype(BF)
 
+    def head_out(h, carry):
+        hs = pl.ds(pl.multiple_of(h * TOK, TOK), TOK)
+        part[OUT].g[hs, :] = dot_tn(s.mixed[:, hs], da).astype(BF)
+        return carry
+
+    lax.fori_loop(0, HEADS, head_out, 0)
+    remote(part[OUT].g.at[rows((1 - me.k) * 512, 512)], part[OUT].r0, (OUT, D1), sibling)
+
     def head_backward(h, carry):
         hs = pl.ds(pl.multiple_of(h * TOK, TOK), TOK)
         dmix = dot_nt(da, part[OUT].w[hs, :]).astype(BF)
@@ -737,51 +759,32 @@
         p = s.probs[hs, :].astype(F32)
         center = jnp.sum(p * d_probs, axis=1, keepdims=True)
         s.ds[hs, :] = (p * (d_probs - center)).astype(BF)
-        for name in (GATE, UP, DOWN):
-            pass_sums(name, h)
         return carry
 
     lax.fori_loop(0, HEADS, head_backward, 0)
 
-    for back in (2, 1, 0):
-        at = slice(back * TOK, back * TOK + TOK)
-        dk = dot_tn(s.ds[:, at], s.qs[...])
-        s.dkv[at, 0:HEAD] = rotate(dk, s.rope[back, 0], -s.rope[back, 1]).astype(BF)
-        s.dkv[at, HEAD:] = dot_tn(s.probs[:, at], s.dmix[...]).astype(BF)
-
-    def swap_halves(n):
-        for b in range(4):
-            remote(
-                part[n].g.at[rows(b * 160 + (1 - me.k) * 80, 80)],
-                part[n].r0.at[pl.ds(b * 80, 80)],
-                (n, D1),
-                sibling,
-            )
-
-    part[2].g[...] = dot_tn(s.xnz[...], s.dkv[...]).astype(BF)
-    swap_halves(2)
-
-    @pl.when((me.zl == 0) & (me.ctx >= 2))
-    def _():
-        remote(block(s.dkv, 1), block(s.dkvr, 0), (DKV, 0), (me.ctx + 1, me.fsdp))
-        remote(block(s.dkv, 2), block(s.dkvr, 2), (DKV, 2), (me.ctx - 2, me.fsdp))
-
-    @pl.when(me.zl == 1)
-    def _():
-        remote(block(s.dkv, 1), block(s.dkvr, 1), (DKV, 1), (me.ctx - 1, me.fsdp))
-
-    def head_query(h, carry):
-        hs = pl.ds(pl.multiple_of(h * TOK, TOK), TOK)
-        dq = dot(s.ds[hs, :], kv[:, 0:HEAD]) * HEAD**-0.5
-        s.dq[:, hs] = rotate(dq, cos, -sin).astype(BF)
-        part[OUT].g[hs, :] = dot_tn(s.mixed[:, hs], da).astype(BF)
-        return carry
-
-    lax.fori_loop(0, HEADS, head_query, 0)
-    for n in (1, 0):
-        part[n].g[...] = dot_tn(s.xn[n], s.dq[:, n * 512 : n * 512 + 512]).astype(BF)
-        swap_halves(n)
-    remote(part[OUT].g.at[rows((1 - me.k) * 512, 512)], part[OUT].r0, (OUT, D1), sibling)
+    def to_blocks(n, starts_of, size):
+        for j in (1, 3, 2):
+            b = around(along(me, LAST[n]), j)
+            for i, start in enumerate(starts_of(b)):
+                remote(
+                    part[n].gs.at[rows(start, size)],
+                    part[n].r1.at[pl.ds(((j - 1) * len(starts_of(b)) + i) * size, size)],
+                    (n, E1),
+                    device(*line_chip(me, LAST[n], j), me.k),
+                )
+
+    def qkv_rows(b):
+        return [b * 80]
+
+    def out_half_rows(b):
+        return [n * 256 + lax.rem(b, 2) * 128 + lax.div(b, 2) * 64 for n in range(2)]
+
+    arrived(part[OUT].r0, (OUT, D1))
+    part[OUT].gs[...] = (
+        part[OUT].g[rows(me.k * 512, 512), :].astype(F32) + part[OUT].r0[...].astype(F32)
+    ).astype(BF)
+    to_blocks(OUT, out_half_rows, 64)
 
     def scatter(n, axis, starts_of, size):
         for j in (1, 3, 2):
@@ -859,22 +862,34 @@
             ).astype(BF)
         scatter(name, *plane_of[name])
 
-    def to_blocks(n, starts_of, size):
-        for j in (1, 3, 2):
-            b = around(along(me, LAST[n]), j)
-            for i, start in enumerate(starts_of(b)):
-                remote(
-                    part[n].gs.at[rows(start, size)],
-                    part[n].r1.at[pl.ds(((j - 1) * len(starts_of(b)) + i) * size, size)],
-                    (n, E1),
-                    device(*line_chip(me, LAST[n], j), me.k),
-                )
-
-    def qkv_rows(b):
-        return [b * 80]
-
-    def out_half_rows(b):
-        return [n * 256 + lax.rem(b, 2) * 128 + lax.div(b, 2) * 64 for n in range(2)]
+    for back in (2, 1, 0):
+        at = slice(back * TOK, back * TOK + TOK)
+        dk = dot_tn(s.ds[:, at], s.qs[...])
+        s.dkv[at, 0:HEAD] = rotate(dk, s.rope[back, 0], -s.rope[back, 1]).astype(BF)
+        s.dkv[at, HEAD:] = dot_tn(s.probs[:, at], s.dmix[...]).astype(BF)
+
+    def swap_halves(n):
+        for b in range(4):
+            remote(
+                part[n].g.at[rows(b * 160 + (1 - me.k) * 80, 80)],
+                part[n].r0.at[pl.ds(b * 80, 80)],
+                (n, D1),
+                sibling,
+            )
+
+    part[2].g[...] = dot_tn(s.xnz[...], s.dkv[...]).astype(BF)
+    swap_halves(2)
+
+    def head_query(h, carry):
+        hs = pl.ds(pl.multiple_of(h * TOK, TOK), TOK)
+        dq = dot(s.ds[hs, :], kv[:, 0:HEAD]) * HEAD**-0.5
+        s.dq[:, hs] = rotate(dq, cos, -sin).astype(BF)
+        return carry
+
+    lax.fori_loop(0, HEADS, head_query, 0)
+    for n in (1, 0):
+        part[n].g[...] = dot_tn(s.xn[n], s.dq[:, n * 512 : n * 512 + 512]).astype(BF)
+        swap_halves(n)
 
     for n in (2, 1, 0):
         arrived(part[n].r0, (n, D1))
@@ -885,11 +900,14 @@
                 + part[n].r0[at, :].astype(F32)
             ).astype(BF)
         to_blocks(n, qkv_rows, 80)
-    arrived(part[OUT].r0, (OUT, D1))
-    part[OUT].gs[...] = (
-        part[OUT].g[rows(me.k * 512, 512), :].astype(F32) + part[OUT].r0[...].astype(F32)
-    ).astype(BF)
-    to_blocks(OUT, out_half_rows, 64)
+    @pl.when((me.zl == 0) & (me.ctx >= 2))
+    def _():
+        remote(block(s.dkv, 1), block(s.dkvr, 0), (DKV, 0), (me.ctx + 1, me.fsdp))
+        remote(block(s.dkv, 2), block(s.dkvr, 2), (DKV, 2), (me.ctx - 2, me.fsdp))
+
+    @pl.when(me.zl == 1)
+    def _():
+        remote(block(s.dkv, 1), block(s.dkvr, 1), (DKV, 1), (me.ctx - 1, me.fsdp))
 
     def owners_same(n, axis):
         home = part[n].rb.at[rows(along(me, axis) * 16, 16)]
@@ -948,9 +966,6 @@
             owners_both(n, XA, lambda place, core: core * 4 + place)
         else:
             owners_low(n, XA if n == OUT else ZA)
-
-    for name in (GATE, UP, DOWN):
-        spread_owners(name)
 
     for n in (2, 1, 0):
         arrived(part[n].r1, (n, E1))
@@ -979,6 +994,9 @@
     part[OUT].gp[:, 256:384] = dot_tn(s.pick8[0], total[:, 256:384]).astype(BF)
     scatter(OUT, *plane_of[OUT])
 
+    for name in (GATE, UP, DOWN):
+        spread_owners(name)
+
     @pl.when((me.zl == 1) & (me.ctx >= 2))
     def _():
         arrived(block(s.dkvr, 0), (DKV, 0))
@@ -988,9 +1006,9 @@
     e0 = dot_nt(s.dq[:, 0:512], part[0].w[...])
     field = dot_nt(s.dq[:, 512:1024], part[1].w[...])
     e0 = e0 + dot_nt(field.astype(BF), s.orders[0])
-    s.ex[0:TOK, :] = e0
+    s.e0[...] = e0
     arrived(s.orecv, OO)
-    lo[...] = s.x1[...] + s.outp[0:TOK, :] + s.orecv[...].astype(F32)
+    lo[...] = s.outp[...] + s.orecv[...].astype(F32)
 
     for n in (2, 1, 0, OUT):
         spread_owners(n)
@@ -1017,7 +1035,7 @@
         + s.dkvr[2 * TOK :, :].astype(F32)
     ).astype(BF)
     field = dot_nt(dkv, part[2].w[...])
-    e0 = s.ex[0:TOK, :] + dot_nt(field.astype(BF), s.orders[1])
+    e0 = s.e0[...] + dot_nt(field.astype(BF), s.orders[1])
     x = s.tokens[0:TOK, :].astype(F32)
     r0 = lax.rsqrt(jnp.mean(x * x, axis=1, keepdims=True) + eps_norm)
     ig[...] = s.dx1[...] + r0 * e0 - x * (r0 * r0 * r0 * jnp.mean(x * e0, axis=1, keepdims=True))

time: 108 us -> 101 us (0.935)
  Pallas kernels: 106 us -> 99.7 us
    pallas_call x1, Pallas kernels: 102 us -> 95.9 us  [whole_step(): pl.pallas_call(functools.partial(step_kernel, scratch), name='whole_step'...]
where the time goes in v3:
time: 101 us
  Pallas kernels  99.7 us (99%)
  between operations  1.47 us (1%)
    pallas_call x1, Pallas kernels, whole_step(): pl.pallas_call(functools.partial(step_kernel, scratch), name='whole_step'...  95.9 us
    pallas_call x1, Pallas kernels, update(): pl.pallas_call(update_kernel, name='update', out_shape=outs, in_specs=[an...  3.8 us

profile of v3, /device:TPU:1, one launch (start us, length us, event | category | flops | bytes accessed | tf_op | source)
XLA Modules:
  0.0 101.2 jit_solution(3301331667875134747)
XLA Ops:
  1.3 95.9 %whole_step.1 = (f32[256,640]{1,0:T(8,128)}, f32[256,640]{1,0:T(8,128)}, f32[16,256]{1,0:T(8,128)}, f32[16,256]{1,0:T(8,128)}, f32[16,256]{1,0:T(8,128)}, /*inde...) custom-call(bf16[1,256,640]{2,1,0:T(8,128)(2,1)} %refs_0_.1, ...), custom_call_target="tpu_custom_call" | custom-call | flops 12000000000 | bytes 8000000 | tf_op jit(solution)/shard_map/whole_step/pallas_call | solution.py:1135
  97.2 3.8 %update.1 = (f32[1,256,640]{2,1,0:T(8,128)}, f32[1,256,640]{2,1,0:T(8,128)}, f32[5,1536]{1,0:T(8,128)}, f32[5,1536]{1,0:T(8,128)}, f32[5,1536]{1,0:T(8,128)}, /*...) custom-call(f32[256,640]{1,0:T(8,128)} %get-tuple-element.26.refs_0_, ...), custom_call_target="tpu_custom_call" | custom-call | tf_op jit(solution)/shard_map/update/pallas_call | solution.py:1236

commit v4 on v3

--- a/solution.py
+++ b/solution.py
@@ -1174,13 +1174,15 @@
     (sq0, sq1, sq2, so, sg, su, sd) = inner[2:9]
     (wq, qf, qs, wo, of, os_, wgu, gf, gs, wd, df, ds_, gains, nf, ns) = inner[9:]
     (oq, oqf, oqs, oo, oof, oos, og, ogf, ogs, od, odf, ods, on, onf, ons) = refs[26:41]
-    for one in copies:
+    for one in copies[:2]:
         one.wait()
     through = [
         pltpu.make_async_copy(inner[n], refs[24 + n].at[0], sem.at[24 + n]) for n in range(2)
     ]
     for one in through:
         one.start()
+    for one in copies[2:]:
+        one.wait()
 
     rate = 1.5 * D**-0.5
     gain0 = column(gains[0:1, :])

time: 101 us -> 101 us (level)
  no operation moved by 1% of the time
where the time goes in v4:
time: 101 us
  Pallas kernels  99.4 us (98%)
  between operations  1.47 us (1%)
    pallas_call x1, Pallas kernels, whole_step(): pl.pallas_call(functools.partial(step_kernel, scratch), name='whole_step'...  95.9 us
    pallas_call x1, Pallas kernels, update(): pl.pallas_call(update_kernel, name='update', out_shape=outs, in_specs=[an...  3.53 us

profile of v4, /device:TPU:1, one launch (start us, length us, event | category | flops | bytes accessed | tf_op | source)
XLA Modules:
  0.0 100.9 jit_solution(3963756829800346337)
XLA Ops:
  1.3 95.9 %whole_step.1 = (f32[256,640]{1,0:T(8,128)}, f32[256,640]{1,0:T(8,128)}, f32[16,256]{1,0:T(8,128)}, f32[16,256]{1,0:T(8,128)}, f32[16,256]{1,0:T(8,128)}, /*inde...) custom-call(bf16[1,256,640]{2,1,0:T(8,128)(2,1)} %refs_0_.1, ...), custom_call_target="tpu_custom_call" | custom-call | flops 12000000000 | bytes 8000000 | tf_op jit(solution)/shard_map/whole_step/pallas_call | solution.py:1135
  97.2 3.5 %update.1 = (f32[1,256,640]{2,1,0:T(8,128)}, f32[1,256,640]{2,1,0:T(8,128)}, f32[5,1536]{1,0:T(8,128)}, f32[5,1536]{1,0:T(8,128)}, f32[5,1536]{1,0:T(8,128)}, /*...) custom-call(f32[256,640]{1,0:T(8,128)} %get-tuple-element.26.refs_0_, ...), custom_call_target="tpu_custom_call" | custom-call | tf_op jit(solution)/shard_map/update/pallas_call | solution.py:1238
